TPU v7x, 512 devices: a whole 4x8x8 slice. The times are simulated.
512 devices in a mesh: outer: 8 (over y), chip: 64 (over z, x, core).
Axes of the slice: x: 4, y: 8, z: 8, core: 2. Of those that a mesh axis runs over, the one named last changes fastest.
Arguments:
- block_input: bfloat16 [8, 24, 24, 1536], P('outer', None, None, 'chip'), may hold values from -6 to 6
- depth_kernel: float32 [7, 7, 1536], replicated, may hold values from -0.875 to 0.875
- w_expand: bfloat16 [1536, 8192], P(None, 'chip'), may hold values from -0.15625 to 0.15625
- grad_hidden: bfloat16 [8, 24, 24, 8192], P('outer', None, None, 'chip'), may hold values from -0.119628906 to 0.119628906
- error_old: float32 [8, 1536, 8192], P('outer', None, 'chip'), may hold values from -3 to 3
- right_init: float32 [8192, 32], P('chip'), may hold values from -6 to 6
Outputs:
- kernel_grad: float32 [7, 7, 1536], P(None, None, 'chip')
- factor_left: float32 [1536, 32], replicated
- factor_right: float32 [8192, 32], P('chip')
- error_new: float32 [8, 1536, 8192], P('outer', None, 'chip')
All inputs are finite; a program needn't handle non-finite values.
Results may differ from a plain program's by a relative error of at most 0.0023.
Values may be sent and summed in bfloat16 or wider, within the bound.
A program may use at most 64 MiB of HBM per device.

v0:
```python
import jax
import jax.numpy as jnp
from jax import lax
from jax.sharding import PartitionSpec as P

HIGH = lax.Precision.HIGHEST


def depthwise(maps, kern):
    half = kern.shape[0] // 2
    side = maps.shape[1]
    padded = jnp.pad(maps, ((0, 0), (half, half), (half, half), (0, 0)))
    total = jnp.zeros(maps.shape, jnp.float32)
    for row in range(kern.shape[0]):
        for col in range(kern.shape[1]):
            total = (
                total
                + padded[:, row : row + side, col : col + side, :].astype(jnp.float32)
                * kern[row, col]
            )
    return total.astype(jnp.bfloat16)


def kernel_terms(maps, grad_conv, ksize):
    half = ksize // 2
    side = maps.shape[1]
    padded = jnp.pad(maps, ((0, 0), (half, half), (half, half), (0, 0)))
    rows = []
    for row in range(ksize):
        cols = []
        for col in range(ksize):
            window = padded[:, row : row + side, col : col + side, :].astype(jnp.float32)
            cols.append(jnp.sum(grad_conv * window, axis=(0, 1, 2)))
        rows.append(jnp.stack(cols))
    return jnp.stack(rows)


def on_device(block_input, depth_kernel, w_expand, grad_hidden, error_old, right_init):
    workers = lax.axis_size("outer")
    ksize = depth_kernel.shape[0]
    width = block_input.shape[3]
    channels = w_expand.shape[0]
    flat_grad = grad_hidden.reshape(-1, grad_hidden.shape[-1])
    grad_part = lax.dot_general(
        flat_grad, w_expand, (((1,), (1,)), ((), ())), preferred_element_type=jnp.float32
    )
    grad_part = grad_part.reshape(block_input.shape[:3] + (channels,))
    offset = lax.axis_index("chip") * width
    kern_shard = lax.dynamic_slice_in_dim(depth_kernel, offset, width, 2)
    conv = depthwise(block_input, kern_shard)
    flat_conv = conv.reshape(-1, width)
    local_grad = lax.dot_general(
        lax.all_gather(flat_conv, "chip", axis=1, tiled=True),
        flat_grad,
        (((0,), (0,)), ((), ())),
        preferred_element_type=jnp.float32,
    )
    grad_share = lax.psum_scatter(grad_part, "chip", scatter_dimension=3, tiled=True)
    kern_term = kernel_terms(block_input, grad_share, ksize)
    kernel_grad = lax.psum(kern_term, "outer")
    corrected = local_grad + error_old[0]
    left_term = jnp.dot(corrected, right_init, precision=HIGH)
    left_sum = lax.psum(left_term, ("outer", "chip"))
    gram = jnp.dot(left_sum.T, left_sum, precision=HIGH)
    chol = jnp.linalg.cholesky(gram)
    factor_left = lax.linalg.triangular_solve(
        chol, left_sum, left_side=False, lower=True, transpose_a=True
    )
    right_term = lax.dot_general(corrected, factor_left, (((0,), (0,)), ((), ())), precision=HIGH)
    factor_right = lax.psum(right_term, "outer")
    approx = jnp.dot(factor_left, factor_right.T, precision=HIGH) / workers
    error_new = (corrected - approx)[None, :, :]
    return (kernel_grad, factor_left, factor_right, error_new)


def solution(mesh):
    placed = (
        P("outer", None, None, "chip"),
        P(),
        P(None, "chip"),
        P("outer", None, None, "chip"),
        P("outer", None, "chip"),
        P("chip", None),
    )
    return jax.shard_map(
        on_device,
        mesh=mesh,
        in_specs=placed,
        out_specs=(P(None, None, "chip"), P(), P("chip", None), P("outer", None, "chip")),
        check_vma=False,
    )
```

profile of v0, /device:TPU:1, one launch (start us, length us, event | category | flops | bytes accessed | tf_op | source)
XLA Modules:
  0.0 617.4 jit_solution(9474245037849300929)
XLA Ops:
  7.2 0.9 copy-done
  8.2 3.4 convolution_bitcast_fusion
  11.6 1.7 fusion.107
  13.4 2.9 fusion.100
  16.3 0.7 copy.11
  17.1 1.3 dynamic-slice
  19.0 202.0 %all-reduce.8.cloned.1.call-done = f32[1,24,24,1536]{3,2,1,0:T(8,128)} async-done(((f32[1,24,24,1536]{3,2,1,0:T(8,128)}), f32[1,24,24,1536]{3,2,1,0:T(8,128)}) %all-reduce.8.cloned.1.call-update) | async-done | bytes 3538960
  221.0 1.9 fusion.99
  222.9 1.8 fusion.97
  224.8 1.9 fusion.98
  226.9 82.0 %all-gather.2.cloned.1.call-done = bf16[576,1536]{0,1:T(8,128)(2,1)} async-done(((bf16[576,24]{0,1:T(8,128)(2,1)}), bf16[576,1536]{0,1:T(8,128)(2,1)}) %all-gather.2.cloned.1.call-update) | async-done | bytes 1769488 | tf_op jit(solution)/shard_map/all_gather | solution.py:53
  308.9 2.2 convolution_add_fusion
  311.2 1.6 fusion.119
  312.8 264.3 %all-reduce.6.cloned.1.call-done = f32[1536,32]{0,1:T(8,128)} async-done(((f32[1536,32]{0,1:T(8,128)}), f32[1536,32]{0,1:T(8,128)}) %all-reduce.6.cloned.1.call-update) | async-done | bytes 196624 | tf_op jit(solution)/shard_map/psum | solution.py:63
  577.0 1.3 fusion.120
  578.4 0.1 copy.12
  578.5 2.9 cholesky.16
  581.4 0.6 compare_reduce_fusion
  582.1 0.7 fusion.102
  582.7 2.4 custom-call.6
  585.2 1.3 fusion.103
  586.5 0.6 fusion.121
  587.0 21.5 %all-reduce.2 = (f32[7,7,24]{2,1,0:T(8,128)}, f32[128,32]{0,1:T(8,128)S(1)}) all-reduce(f32[7,7,24]{2,1,0:T(8,128)S(1)} %constant_dynamic-update-slice_fusion, f32[128,32]{0,1:T(8,128)S(1)} %fusion.121), channel_id=1, replica_groups=mesh['outer'=8,'chip'=64] {'outer'}, use_global_device_ids=true, to_apply=%region_50.51 | all-reduce | flops 5272 | bytes 42176 | tf_op jit(solution)/shard_map/psum | solution.py:60
  608.5 2.3 fusion.1
  (35 shorter events, 0.4 us)
Async XLA Ops:
  7.2 1.0 copy-start
  7.2 6.2 %copy-start.1 = (bf16[1,24,24,24]{3,2,1,0:T(8,128)(2,1)S(1)}, bf16[1,24,24,24]{3,2,1,0:T(8,128)(2,1)}, u32[]{:S(2)}) copy-start(bf16[1,24,24,24]{3,2,1,0:T(8,128)(2,1)} %param.6) | copy-start | bytes 82948
  7.2 213.8 %all-reduce.8.cloned.1.call-start = ((), (), s32[]{:S(2)}) async-start(), calls=%async_computation.2 | async-start | bytes 7077888
  11.5 297.4 %copy-start.3 = (f32[1,1536,128]{2,1,0:T(8,128)S(1)}, f32[1,1536,128]{2,1,0:T(8,128)}, u32[]{:S(2)}) copy-start(f32[1,1536,128]{2,1,0:T(8,128)} %param.10) | copy-start | bytes 2359300
  11.5 297.4 %copy-start.4 = (bf16[1,24,24,128]{3,2,1,0:T(8,128)(2,1)S(1)}, bf16[1,24,24,128]{3,2,1,0:T(8,128)(2,1)}, u32[]{:S(2)}) copy-start(bf16[1,24,24,128]{3,2,1,0:T(8,128)(2,1)} %param.9) | copy-start | bytes 442372
  11.6 299.6 %copy-start.5 = (f32[128,32]{0,1:T(8,128)S(1)}, f32[128,32]{0,1:T(8,128)}, u32[]{:S(2)}) copy-start(f32[128,32]{0,1:T(8,128)} %param.11) | copy-start | bytes 49156
  11.6 297.3 %all-gather.2.cloned.1.call-start = ((), (), s32[]{:S(2)}) async-start(), calls=%async_computation | async-start | bytes 1996800 | tf_op jit(solution)/shard_map/all_gather | solution.py:53
  17.1 560.0 %all-reduce.6.cloned.1.call-start = ((), (), s32[]{:S(2)}) async-start(), calls=%async_computation.1 | async-start | bytes 393216 | tf_op jit(solution)/shard_map/psum | solution.py:63
  586.5 24.4 %copy-start.2 = (f32[1536,32]{0,1:T(8,128)}, f32[1536,32]{0,1:T(8,128)S(1)}, u32[]{:S(2)}) copy-start(f32[1536,32]{0,1:T(8,128)S(1)} %fusion.103) | copy-start | bytes 589828
  608.5 2.3 copy-start.6
Sparse Core Ops, SparseCore 0:
  11.7 209.2 all-reduce.7
  225.3 83.5 all-gather.1
  315.2 261.7 all-reduce.5
where the time goes:
time: 624 us; the launch traced here: 617 us
  waiting for transfers between devices  548 us (88%)
  blocking collectives  21.5 us (3%)
  other arithmetic  15.3 us (2%)
  between operations  14.6 us (2%)
  matrix products  12.7 us (2%)
    psum x1, waiting for transfers between devices, on_device(): left_sum = lax.psum(left_term, ('outer', 'chip'))  264 us
    unnamed x4, waiting for transfers between devices  202 us
    all_gather x1, waiting for transfers between devices, on_device(): lax.all_gather(flat_conv, 'chip', axis=1, tiled=True)  82 us
    psum x1, blocking collectives, on_device(): kernel_grad = lax.psum(kern_term, 'outer')  21.5 us
  transfers between devices with their start and end apart: 3, of which 3 were waited for; matrix products, arithmetic and copies ran while one was open for 2% of the time, Pallas kernels for 0%

commit v1 on v0

v1 whole, which is shorter than its diff:
```python
import functools

import jax
import jax.numpy as jnp
from jax import lax
from jax.experimental import pallas as pl
from jax.experimental.pallas import tpu as pltpu
from jax.sharding import PartitionSpec as P

F32 = jnp.float32
BF16 = jnp.bfloat16
HIGH = lax.Precision.HIGHEST
MESH = pl.DeviceIdType.MESH

NX = 4
SIDE = 24
POS = SIDE * SIDE
LP = 640
LX = 896
OWN = 24
RANK = 32


def dot(a, b, dims, precision=None):
    return lax.dot_general(a, b, (dims, ((), ())), precision=precision, preferred_element_type=F32)


NN = ((1,), (0,))
NT = ((1,), (1,))
TN = ((0,), (0,))


def loop(lo, hi, body, unroll=1):
    def step(i, carry):
        body(i)
        return carry

    lax.fori_loop(lo, hi, step, 0, unroll=unroll)


def split2(v):
    hi = v.astype(BF16)
    return hi, (v - hi.astype(F32)).astype(BF16)


def split3(v):
    hi = v.astype(BF16)
    rest = v - hi.astype(F32)
    mid = rest.astype(BF16)
    return hi, mid, (rest - mid.astype(F32)).astype(BF16)


def kernel(
    ny, nz, nx,
    x_hbm, k_hbm, w_hbm, gh_hbm, err_hbm, r_hbm,
    kg_out, left_out, right_out, w_out, ls4, cor,
    x_ref, k_ref, w_ref, err_ref, r_ref,
    ghp, ghs, ws, rs, wf, x2, xz, xp, xs, mk, kflat, kt, conv32, cvf, gr, gb, rh1, rh2, g32,
    eg, gg, es, cs, gt, st, rz, ys, ll, chl, rp, kgt, rk, yk, lsn,
    s_in,
    s_xz, r_xz, s_es, r_es, s_cs, r_cs, s_gt, r_gt, s_rz, r_rz, s_ys, r_ys, s_lx, r_lx, s_lz, r_lz,
    s_lk, r_lk, s_rp, r_rp, s_rk, r_rk, s_yk, r_yk, s_in2, r_in2, s_gx, r_gx, s_cx, r_cx, s_cc, r_cc,
):
    nxk = 2 * nx
    ch = OWN * nz
    channels = ch * nxk
    tpz = 8 // nz
    half = ch // 2
    workers = ny
    y = lax.axis_index("outer")
    chip = lax.axis_index("chip")
    z = chip // nxk
    xk = lax.rem(chip, nxk)
    x = xk // 2
    k = lax.rem(xk, 2)

    def zpeer(s):
        return lax.rem(z + s, nz)

    def at_z(zz):
        return (y, zz * nxk + xk)

    def at_x(xx):
        return (y, z * nxk + xx * 2 + k)

    right_x = lax.rem(x + 1, nx)
    left_x = lax.rem(x + nx - 1, nx)
    far_x = lax.rem(x + 2, nx)

    def at_y(yy):
        return (yy, chip)

    sibling = (y, z * nxk + x * 2 + (1 - k))

    def copy(src, dst, ssem, rsem, dev):
        return pltpu.make_async_remote_copy(
            src_ref=src, dst_ref=dst, send_sem=ssem, recv_sem=rsem,
            device_id=dev, device_id_type=MESH,
        )

    load_x = pltpu.make_async_copy(x_hbm, x_ref, s_in.at[0])
    load_r = pltpu.make_async_copy(r_hbm, r_ref, s_in.at[1])
    load_err = pltpu.make_async_copy(err_hbm, err_ref, s_in.at[2])
    load_gh = pltpu.make_async_copy(gh_hbm, ghp.at[pl.ds(0, POS)], s_in.at[3])
    load_w = pltpu.make_async_copy(w_hbm, w_ref, s_in.at[4])
    load_k = pltpu.make_async_copy(k_hbm, k_ref, s_in.at[5])
    for load in (load_x, load_r, load_err, load_gh, load_w, load_k):
        load.start()

    barrier = pltpu.get_barrier_semaphore()

    def greet(dev):
        pl.semaphore_signal(barrier, inc=1, device_id=dev, device_id_type=MESH)

    loop(1, nz, lambda s: greet(at_z(zpeer(s))))
    loop(1, nx, lambda s: greet(at_x(lax.rem(x + s, nx))))
    greet(sibling)
    loop(1, ny, lambda s: greet(at_y(lax.rem(y + s, ny))))

    x2[...] = jnp.zeros((3, LX, OWN), F32)
    load_x.wait()
    for i in range(SIDE):
        image_row = x_ref[i].astype(F32)
        x2[0, SIDE * i : SIDE * (i + 1), :] = image_row
        late = i >= SIDE // 2
        at = POS + SIDE * (i % (SIDE // 2))
        x2[2 if late else 1, at : at + SIDE, :] = image_row
    out_row = lax.broadcasted_iota(jnp.int32, (16, OWN), 0)
    channel = lax.broadcasted_iota(jnp.int32, (16, OWN), 1)
    picks = (
        channel == out_row,
        (channel == out_row + 16) & (out_row < 8),
        (channel == out_row + 8) & (out_row >= 8),
    )
    packed = None
    for j in range(3):
        term = dot(picks[j].astype(F32).astype(BF16), x2[j].astype(BF16), NT)
        packed = term if packed is None else packed + term
    xz[z] = packed.astype(BF16)
    ghp[POS:, :] = jnp.zeros((LP - POS, 128), BF16)
    ghs[POS:, :] = jnp.zeros((LP - POS, 128), BF16)

    load_r.wait()
    load_err.wait()
    rh, rl = split2(r_ref[...])
    four = jnp.concatenate(
        [jnp.concatenate([rh, rh], axis=1), jnp.concatenate([rl, rl], axis=1)], axis=0
    )
    for q in range(nxk):
        eh, el = split2(err_ref[:, q].reshape(ch, 128))
        rows = jnp.concatenate([eh, el], axis=1)
        if ch < 256:
            rows = jnp.concatenate([rows, jnp.zeros((256 - ch, 256), BF16)], axis=0)
        e = dot(four, rows, NT)
        e = e[0:32] + e[32:64]
        for rg in range(4):
            for part in range(2):
                eg[q // 2, q % 2, 2 * rg + part] = e[8 * rg : 8 * rg + 8, 128 * part : 128 * part + 128]

    pl.semaphore_wait(barrier, (nz - 1) + (nx - 1) + (ny - 1) + 1)

    es_copy = copy(eg.at[:, 1 - k], es, s_es.at[0], r_es.at[0], sibling)
    in_gh = copy(gh_hbm, ghs.at[pl.ds(0, POS)], s_in2.at[0], r_in2.at[0], sibling)
    in_r = copy(r_hbm, rs, s_in2.at[1], r_in2.at[1], sibling)
    in_w = copy(w_hbm, ws, s_in2.at[2], r_in2.at[2], sibling)

    def xz_copy(s):
        return copy(xz.at[z], xz.at[z], s_xz.at[s], r_xz.at[s], at_z(zpeer(s)))

    loop(1, nz, lambda s: xz_copy(s).start())
    for one in (in_r, in_gh, es_copy, in_w):
        one.start()

    load_k.wait()
    for a in range(7):
        kflat[8 * a : 8 * a + 7, :] = k_ref[a]
        kflat[8 * a + 7 : 8 * a + 8, :] = jnp.zeros((1, channels), F32)
    kflat[56:64, :] = jnp.zeros((8, channels), F32)
    row = lax.broadcasted_iota(jnp.int32, (OWN, channels), 0)
    lane = lax.broadcasted_iota(jnp.int32, (OWN, channels), 1)
    apart = lane - row - xk * OWN
    pick = jnp.concatenate([(apart == zz * nxk * OWN).astype(F32) for zz in range(nz)], axis=0)
    three = jnp.concatenate(split3(kflat[...]), axis=0)
    taps3 = dot(pick.astype(BF16), three, NT)
    kt[...] = taps3[:, 0:64] + taps3[:, 64:128] + taps3[:, 128:192]
    pos = lax.broadcasted_iota(jnp.int32, (8, LP), 1)
    col = lax.rem(pos, SIDE) + lax.broadcasted_iota(jnp.int32, (8, LP), 0) - 3
    mk[...] = ((col >= 0) & (col < SIDE) & (pos < POS)).astype(F32)
    xp[:, 0:128] = jnp.zeros((ch, 128), F32)
    xp[:, 128 + LP :] = jnp.zeros((ch, LX - 128 - LP), F32)

    load_gh.wait()
    in_gh.wait_recv()
    in_r.wait_recv()
    sh, sl = split2(rs[...])
    both = jnp.concatenate([ghp[...], ghs[...]], axis=1)
    g = dot(
        jnp.concatenate([rh, sh, rl, sl], axis=1), jnp.concatenate([both, both], axis=1), NT
    )
    for rg in range(4):
        for j in range(5):
            gg[rg // 2, (rg % 2) * 5 + j] = g[8 * rg : 8 * rg + 8, 128 * j : 128 * j + 128]

    es_copy.wait_recv()

    def chip_sum(xx):
        cs[xx, 0, 0:8] = eg[xx, k] + es[xx]
        cs[xx, 0, 8:18] = gg[k]

    loop(0, nx, chip_sum)
    cs[x, 1] = cs[x, 0]

    def cs_copy(s):
        xx = lax.rem(x + s, nx)
        return copy(cs.at[xx, 0], cs.at[x, 1], s_cs.at[s], r_cs.at[s], at_x(xx))

    loop(1, nx, lambda s: cs_copy(s).start())

    load_w.wait()
    in_w.wait_recv()
    wf[:, :, :, :, 0:128] = w_ref[...].astype(F32).reshape(nz, nx, 2, OWN, 128)
    wf[:, :, :, :, 128:256] = ws[...].astype(F32).reshape(nz, nx, 2, OWN, 128)

    def grad_rows(xx):
        rows = wf[:, xx, k].reshape(ch, 256).astype(BF16)
        return dot(rows, jnp.concatenate([ghp[...], ghs[...]], axis=1), NT)

    gb[0] = grad_rows(far_x).astype(BF16)
    far_right = copy(
        gb.at[0, pl.ds(0, half)], rh1.at[0], s_gx.at[0], r_gx.at[0], at_x(right_x)
    )
    far_left = copy(
        gb.at[0, pl.ds(half, half)], rh1.at[1], s_gx.at[1], r_gx.at[1], at_x(left_x)
    )
    far_right.start()
    far_left.start()
    gr[0] = grad_rows(right_x)
    gr[1] = grad_rows(left_x)
    g32[...] = grad_rows(x)

    loop(1, nx, lambda s: cs_copy(s).wait_recv())
    total = cs[0, 1]
    for q in range(1, nx):
        total = total + cs[q, 1]
    st[...] = total[0:8]
    gt[k] = total[8:18]
    gt_copy = copy(gt.at[k], gt.at[k], s_gt.at[0], r_gt.at[0], sibling)
    gt_copy.start()

    loop(1, nz, lambda s: xz_copy(s).wait_recv())
    lane_x = lax.broadcasted_iota(jnp.int32, (16, LX), 1)
    for zz in range(nz):
        v = xz[zz].astype(F32)
        xp[OWN * zz : OWN * zz + 16, 128 : 128 + LP] = jnp.where(lane_x < POS, v, 0.0)[:, 0:LP]
        early = pltpu.roll(v[0:8], LX - POS, 1)
        late = pltpu.roll(v[8:16], LX - POS // 2, 1)
        last = jnp.where(
            lane_x[0:8] < POS // 2, early, jnp.where(lane_x[0:8] < POS, late, 0.0)
        )
        xp[OWN * zz + 16 : OWN * zz + 24, 128 : 128 + LP] = last[:, 0:LP]

    def conv_rows(t):
        rows = pl.ds(pl.multiple_of(t * 8, 8), 8)
        v = xp[rows, :]
        taps = kt[rows, :]
        moved = [pltpu.roll(v, LX - (96 + SIDE * (a - 3)), 1)[:, 0:LP] for a in range(7)]
        for a in range(7):
            xs[a, rows, :] = moved[a]
        out = None
        for b in range(7):
            part = None
            for a in range(7):
                term = taps[:, 8 * a + b : 8 * a + b + 1] * moved[a]
                part = term if a == 0 else part + term
            part = pltpu.roll(part, LP - (32 + b - 3), 1) * mk[b : b + 1, :]
            out = part if b == 0 else out + part
        conv32[rows, :] = out

    loop(0, ch // 8, conv_rows, 2)
    cvf[x, k] = conv32[...].astype(BF16)

    mine = cvf.at[x, k]
    cx_copies = [
        copy(mine, mine, s_cx.at[0], r_cx.at[0], at_x(right_x)),
        copy(mine, mine, s_cx.at[1], r_cx.at[1], at_x(left_x)),
    ]
    for s in range(2):
        cx_copies[s].start()

    sources = (x, left_x, right_x, far_x)

    def cc_copy(s):
        block = cvf.at[sources[s], k]
        return copy(block, block, s_cc.at[s], r_cc.at[s], sibling)

    cc_copy(0).start()

    gt_copy.wait_recv()
    groups = []
    for rg in range(4):
        groups.append(
            jnp.concatenate([gt[rg // 2, (rg % 2) * 5 + j] for j in range(5)], axis=1)
        )
    gsplit = jnp.concatenate(split2(jnp.concatenate(groups, axis=0)), axis=0)
    conv_pad = cvf[x, k]
    if ch < 256:
        conv_pad = jnp.concatenate([conv_pad, jnp.zeros((256 - ch, LP), BF16)], axis=0)
    left = dot(gsplit, conv_pad, NT)
    left = left[0:32] + left[32:64]
    for rg in range(4):
        for part in range(2):
            st[2 * rg + part] += left[8 * rg : 8 * rg + 8, 128 * part : 128 * part + 128]

    def rz_copy(s):
        zz = zpeer(s)
        return copy(st.at[pl.ds(zz * tpz, tpz)], rz.at[z], s_rz.at[s], r_rz.at[s], at_z(zz))

    loop(1, nz, lambda s: rz_copy(s).start())
    rz[z] = st[pl.ds(z * tpz, tpz)]

    far_right.wait_recv()
    gb[1, 0:half, :] = (gr[0, 0:half, :] + rh1[0].astype(F32)).astype(BF16)
    gb[1, half:, :] = gr[0, half:, :].astype(BF16)
    near_right = copy(gb.at[1], rh2.at[0], s_gx.at[2], r_gx.at[2], at_x(right_x))
    near_right.start()
    far_left.wait_recv()
    gb[2, 0:half, :] = gr[1, 0:half, :].astype(BF16)
    gb[2, half:, :] = (gr[1, half:, :] + rh1[1].astype(F32)).astype(BF16)
    near_left = copy(gb.at[2], rh2.at[1], s_gx.at[3], r_gx.at[3], at_x(left_x))
    near_left.start()

    loop(1, nz, lambda s: rz_copy(s).wait_recv())
    total = rz[0]
    for q in range(1, nz):
        total = total + rz[q]
    ys[y] = total

    def ys_copy(s):
        return copy(ys.at[y], ys.at[y], s_ys.at[s], r_ys.at[s], at_y(lax.rem(y + s, ny)))

    loop(1, ny, lambda s: ys_copy(s).start())

    def local_grad(xx, kk):
        q = xx * 2 + kk
        part = dot(cvf[xx, kk], ghp[...], NN) + err_ref[:, q].reshape(ch, 128)
        cor[:, q] = part.reshape(nz, OWN, 128)
        chl[q, 0:ch, :] = jnp.concatenate(split2(part), axis=1)

    if ch < 256:
        chl[:, ch:, :] = jnp.zeros((nxk, 256 - ch, 256), BF16)
    local_grad(x, k)

    loop(1, ny, lambda s: ys_copy(s).wait_recv())
    total = ys[0]
    for q in range(1, ny):
        total = total + ys[q]
    ll[k, z, x] = total

    def lx_copy(s):
        own = ll.at[k, z, x]
        return copy(own, own, s_lx.at[s], r_lx.at[s], at_x(lax.rem(x + s, nx)))

    loop(1, nx, lambda s: lx_copy(s).start())

    cx_copies[0].wait_recv()
    part0 = cvf.at[left_x, k, pl.ds(0, half)]
    cx_copies.append(copy(part0, part0, s_cx.at[2], r_cx.at[2], at_x(right_x)))
    cx_copies[2].start()
    cc_copy(1).start()
    cx_copies[1].wait_recv()
    part1 = cvf.at[right_x, k, pl.ds(half, half)]
    cx_copies.append(copy(part1, part1, s_cx.at[3], r_cx.at[3], at_x(left_x)))
    cx_copies[3].start()
    cc_copy(2).start()
    local_grad(left_x, k)
    local_grad(right_x, k)

    def lx_wait(s):
        got = ll.at[k, z, lax.rem(x - s + nx, nx)]
        copy(got, got, s_lx.at[s], r_lx.at[s], at_x(lax.rem(x + s, nx))).wait_recv()

    loop(1, nx, lx_wait)

    def lz_copy(s):
        own = ll.at[k, z]
        return copy(own, own, s_lz.at[s], r_lz.at[s], at_z(zpeer(s)))

    loop(1, nz, lambda s: lz_copy(s).start())
    for s in range(3):
        cc_copy(s).wait_recv()
        local_grad(sources[s], 1 - k)

    def lz_wait(s):
        got = ll.at[k, lax.rem(z - s + nz, nz)]
        copy(got, got, s_lz.at[s], r_lz.at[s], at_z(zpeer(s))).wait_recv()

    near_right.wait_recv()
    near_left.wait_recv()
    g32[...] += rh2[0].astype(F32) + rh2[1].astype(F32)
    lane128 = lax.broadcasted_iota(jnp.int32, (8, 128), 1)

    def kernel_terms(t):
        rows = pl.ds(pl.multiple_of(t * 8, 8), 8)
        gt = g32[rows, :]
        out = jnp.zeros((8, 128), F32)
        for b in range(7):
            gm = pltpu.roll(gt * mk[b : b + 1, :], 32 + b - 3, 1)
            for a in range(7):
                one = jnp.sum(gm * xs[a, rows, :], axis=1, keepdims=True)
                out = jnp.where(lane128 == 7 * a + b, one, out)
        kgt[t // 3, pl.ds(pl.multiple_of(lax.rem(t, 3) * 8, 8), 8), :] = out

    loop(0, ch // 8, kernel_terms, 2)

    def rk_copy(s):
        zz = zpeer(s)
        return copy(kgt.at[zz], rk.at[z], s_rk.at[s], r_rk.at[s], at_z(zz))

    loop(1, nz, lambda s: rk_copy(s).start())
    rk[z] = kgt[z]

    loop(1, nz, lz_wait)
    lk_copy = copy(ll.at[k], ll.at[k], s_lk.at[0], r_lk.at[0], sibling)
    lk_copy.start()

    cx_copies[2].wait_recv()
    cx_copies[3].wait_recv()
    cc_copy(3).start()
    local_grad(far_x, k)
    lk_copy.wait_recv()

    def left_of(q):
        rows = []
        for rg in range(4):
            tiles = [ll[q % 2, t // tpz, q // 2, t % tpz] for t in (2 * rg, 2 * rg + 1)]
            rows.append(jnp.concatenate(tiles, axis=1))
        return jnp.concatenate(rows, axis=0)

    lefts = [left_of(q) for q in range(nxk)]
    wide3 = split3(jnp.concatenate(lefts, axis=1))
    stack3 = jnp.concatenate(wide3, axis=0)
    gram = None
    for part in wide3:
        term = dot(stack3, part, NT)
        term = term[0:32] + term[32:64] + term[64:96]
        gram = term if gram is None else gram + term
    for q in range(nxk):
        lsn[:, q] = lefts[q].T[0:ch].reshape(nz, OWN, RANK)
    natural = lsn[...].reshape(channels, RANK).T
    nh, nm, nl = split3(natural)
    ls4[...] = jnp.concatenate([nh, nm, nh, nm], axis=0).T

    row_id = lax.broadcasted_iota(jnp.int32, (RANK, RANK), 0)
    lane_id = lax.broadcasted_iota(jnp.int32, (RANK, RANK), 1)
    same = row_id == lane_id
    aug = jnp.concatenate([gram, same.astype(F32)], axis=1)
    row_col = lax.broadcasted_iota(jnp.int32, (RANK, 2 * RANK), 0)

    def full(v):
        return jnp.broadcast_to(v, (RANK, 2 * RANK))

    for i in range(0, RANK, 2):
        c0 = full(aug[:, i : i + 1])
        c1 = full(aug[:, i + 1 : i + 2])
        r0 = full(aug[i : i + 1, :])
        r1 = full(aug[i + 1 : i + 2, :])
        p00 = full(c0[i : i + 1, :])
        p01 = full(c1[i : i + 1, :])
        p11 = full(c1[i + 1 : i + 2, :])
        inv = 1.0 / (p00 * p11 - p01 * p01)
        u0 = (p11 * c0 - p01 * c1) * inv
        u1 = (p00 * c1 - p01 * c0) * inv
        u0 = jnp.where(row_col > i + 1, u0, jnp.where(row_col == i + 1, p01 / p00, 0.0))
        u1 = jnp.where(row_col > i + 1, u1, 0.0)
        aug = aug - u0 * r0 - u1 * r1
    diag = jnp.sum(jnp.where(same, aug[:, 0:RANK], 0.0), axis=1, keepdims=True)
    scale = lax.rsqrt(diag)
    scale = scale * (1.5 - 0.5 * diag * scale * scale)
    linv = aug[:, RANK:] * scale
    ih, im, il = split3(linv)
    left_out[...] = dot(
        jnp.concatenate([ih, ih, ih, im, im, il], axis=1),
        jnp.concatenate([nh, nm, nl, nh, nm, nh], axis=0),
        NN,
    )

    cc_copy(3).wait_recv()
    local_grad(far_x, 1 - k)

    loop(1, nz, lambda s: rk_copy(s).wait_recv())
    total = rk[0]
    for q in range(1, nz):
        total = total + rk[q]
    yk[y] = total

    def yk_copy(s):
        return copy(yk.at[y], yk.at[y], s_yk.at[s], r_yk.at[s], at_y(lax.rem(y + s, ny)))

    loop(1, ny, lambda s: yk_copy(s).start())

    right = None
    for q in range(nxk):
        term = dot(jnp.concatenate(split2(left_of(q)), axis=0), chl[q], NN)
        right = term if q == 0 else right + term
    right = right[0:32] + right[32:64]
    rp[y] = right[:, 0:128] + right[:, 128:256]

    def rp_copy(s):
        return copy(rp.at[y], rp.at[y], s_rp.at[s], r_rp.at[s], at_y(lax.rem(y + s, ny)))

    loop(1, ny, lambda s: rp_copy(s).start())

    loop(1, ny, lambda s: rp_copy(s).wait_recv())
    total = rp[0]
    for q in range(1, ny):
        total = total + rp[q]
    fright = dot(linv, total, NN, HIGH)
    right_out[...] = fright
    wh, wl = split2(dot(linv.T, fright, NN, HIGH) * (1.0 / workers))
    w_out[...] = jnp.concatenate([wh, wh, wl, wl], axis=0)

    loop(1, ny, lambda s: yk_copy(s).wait_recv())
    total = yk[0]
    for q in range(1, ny):
        total = total + yk[q]
    total = total.T
    for a in range(7):
        kg_out[a] = total[7 * a : 7 * a + 7]

    loop(1, nz, lambda s: xz_copy(s).wait_send())
    es_copy.wait_send()
    for one in (in_r, in_gh, in_w):
        one.wait_send()
    loop(1, nx, lambda s: cs_copy(s).wait_send())
    gt_copy.wait_send()
    loop(1, nz, lambda s: rz_copy(s).wait_send())
    loop(1, ny, lambda s: ys_copy(s).wait_send())
    loop(1, nx, lambda s: lx_copy(s).wait_send())
    loop(1, nz, lambda s: lz_copy(s).wait_send())
    lk_copy.wait_send()
    loop(1, ny, lambda s: rp_copy(s).wait_send())
    loop(1, nz, lambda s: rk_copy(s).wait_send())
    loop(1, ny, lambda s: yk_copy(s).wait_send())
    for s in range(4):
        cx_copies[s].wait_send()
        cc_copy(s).wait_send()
    for one in (far_right, far_left, near_right, near_left):
        one.wait_send()


def finish(kg_ref, left_ref, right_ref, w_ref, ls_ref, cor_ref, kg_out, left_out, right_out, err_out):
    kg_out[...] = kg_ref[...]
    left_out[...] = left_ref[...]
    right_out[...] = right_ref[...]
    approx = dot(ls_ref[...], w_ref[...], NN)
    err_out[...] = cor_ref[...] - approx.reshape(cor_ref.shape)


def on_device(ny, nz, nx, block_input, depth_kernel, w_expand, grad_hidden, error_old, right_init):
    nxk = 2 * nx
    ch = OWN * nz
    channels = nz * nxk * OWN
    tpz = 8 // nz
    hid = right_init.shape[0]
    vmem = pltpu.VMEM
    scratch = [
        vmem((SIDE, SIDE, OWN), BF16),
        vmem((7, 7, channels), F32),
        vmem((channels, 128), BF16),
        vmem((nz, nxk, OWN, 128), F32),
        vmem((RANK, 128), F32),
        vmem((LP, 128), BF16),
        vmem((LP, 128), BF16),
        vmem((channels, 128), BF16),
        vmem((RANK, 128), F32),
        vmem((nz, nx, 2, OWN, 256), F32),
        vmem((3, LX, OWN), F32),
        vmem((nz, 16, LX), BF16),
        vmem((ch, LX), F32),
        vmem((7, ch, LP), F32),
        vmem((8, LP), F32),
        vmem((64, channels), F32),
        vmem((ch, 64), F32),
        vmem((ch, LP), F32),
        vmem((nx, 2, ch, LP), BF16),
        vmem((2, ch, LP), F32),
        vmem((3, ch, LP), BF16),
        vmem((2, ch // 2, LP), BF16),
        vmem((2, ch, LP), BF16),
        vmem((ch, LP), F32),
        vmem((nx, 2, 8, 8, 128), F32),
        vmem((2, 10, 8, 128), F32),
        vmem((nx, 8, 8, 128), F32),
        vmem((nx, 2, 18, 8, 128), F32),
        vmem((2, 10, 8, 128), F32),
        vmem((8, 8, 128), F32),
        vmem((nz, tpz, 8, 128), F32),
        vmem((ny, tpz, 8, 128), F32),
        vmem((2, nz, nx, tpz, 8, 128), F32),
        vmem((nxk, 256, 256), BF16),
        vmem((ny, RANK, 128), F32),
        vmem((nz, OWN, 128), F32),
        vmem((nz, OWN, 128), F32),
        vmem((ny, OWN, 128), F32),
        vmem((nz, nxk, OWN, RANK), F32),
    ]
    sems = [pltpu.SemaphoreType.DMA((6,))]
    for count in (nz, 2, nx, 1, nz, ny, nx, nz, 1, ny, nz, ny, 4, 4, 4, 4):
        sems += [pltpu.SemaphoreType.DMA((count,))] * 2
    spec = pl.BlockSpec(memory_space=pltpu.VMEM)
    cor_shape = jax.ShapeDtypeStruct((nz, nxk, OWN, 128), F32)
    mids = (
        jax.ShapeDtypeStruct((7, 7, OWN), F32),
        jax.ShapeDtypeStruct((RANK, channels), F32),
        jax.ShapeDtypeStruct((RANK, 128), F32),
        jax.ShapeDtypeStruct((4 * RANK, 128), BF16),
        jax.ShapeDtypeStruct((channels, 4 * RANK), BF16),
        cor_shape,
    )
    parts = pl.pallas_call(
        functools.partial(kernel, ny, nz, nx),
        out_shape=mids,
        in_specs=[pl.BlockSpec(memory_space=pl.ANY)] * 6,
        out_specs=(spec,) * 6,
        scratch_shapes=scratch + sems,
        compiler_params=pltpu.CompilerParams(
            collective_id=0, has_side_effects=True, vmem_limit_bytes=60 * 1024 * 1024
        ),
        cost_estimate=pl.CostEstimate(
            flops=600_000_000, bytes_accessed=4_000_000, transcendentals=0
        ),
    )(
        block_input.reshape(SIDE, SIDE, OWN),
        depth_kernel,
        w_expand,
        grad_hidden.reshape(POS, 128),
        error_old.reshape(nz, nxk, OWN, 128),
        right_init.T,
    )
    kg, left, right, err = pl.pallas_call(
        finish,
        out_shape=mids[0:3] + (cor_shape,),
        in_specs=[spec] * 6,
        out_specs=(spec,) * 4,
        compiler_params=pltpu.CompilerParams(vmem_limit_bytes=60 * 1024 * 1024),
        cost_estimate=pl.CostEstimate(
            flops=60_000_000, bytes_accessed=2_500_000, transcendentals=0
        ),
    )(*parts)
    return (
        kg,
        left.T,
        right.T,
        err.reshape(1, channels, 128),
    )


def solution(mesh, nx=NX):
    ny = mesh.shape["outer"]
    nz = mesh.shape["chip"] // (2 * nx)
    placed = (
        P("outer", None, None, "chip"),
        P(),
        P(None, "chip"),
        P("outer", None, None, "chip"),
        P("outer", None, "chip"),
        P("chip", None),
    )
    return jax.shard_map(
        functools.partial(on_device, ny, nz, nx),
        mesh=mesh,
        in_specs=placed,
        out_specs=(P(None, None, "chip"), P(), P("chip", None), P("outer", None, "chip")),
        check_vma=False,
    )
```

time: 624 us -> 80.2 us (0.13)
  waiting for transfers between devices: 548 us -> 0 us
  Pallas kernels: 0 us -> 78.5 us
  blocking collectives: 21.5 us -> 0 us
  other arithmetic: 15.3 us -> 0 us
  between operations: 14.6 us -> 0.64 us
  matrix products: 12.7 us -> 0 us
    psum x1 -> x0, waiting for transfers between devices: 264 us -> none  [on_device(): left_sum = lax.psum(left_term, ('outer', 'chip'))]
    unnamed x4 -> x0, waiting for transfers between devices: 202 us -> none
    all_gather x1 -> x0, waiting for transfers between devices: 82 us -> none  [on_device(): lax.all_gather(flat_conv, 'chip', axis=1, tiled=True)]
    pallas_call x0 -> x2, Pallas kernels: none -> 78.5 us  [the longest x1 75.9 us: on_device(): pl.pallas_call(functools.partial(kernel, ny, nz, nx), out_shape=mids, in_...]
    psum x1 -> x0, blocking collectives: 21.5 us -> none  [on_device(): kernel_grad = lax.psum(kern_term, 'outer')]
    dot_general x6 -> x0, matrix products: 11.3 us -> none  [the longest x1 3.38 us: on_device(): lax.dot_general(flat_grad, w_expand, (((1,), (1,)), ((), ())), preferred_...]
    another operation x5 -> x0, other arithmetic: 6.68 us -> none  [the longest x3 3.6 us: on_device(): chol = jnp.linalg.cholesky(gram)]
  transfers between devices with their start and end apart: 3 -> 0, of which waited for: 3 -> 0; matrix products, arithmetic and copies ran while one was open for 2% -> 0% of each run, Pallas kernels for 0% -> 0%
where the time goes in v1:
time: 80.2 us; the launch traced here: 79.1 us
  Pallas kernels  78.5 us (98%)
    pallas_call x1, Pallas kernels, on_device(): pl.pallas_call(functools.partial(kernel, ny, nz, nx), out_shape=mids, in_...  75.9 us
    pallas_call x1, Pallas kernels, on_device(): pl.pallas_call(finish, out_shape=mids[0:3] + (cor_shape,), in_specs=[spec...  2.58 us

profile of v1, /device:TPU:1, one launch (start us, length us, event | category | flops | bytes accessed | tf_op | source)
XLA Modules:
  0.0 79.1 jit_solution(14409227365950627151)
XLA Ops:
  0.6 75.9 %shard_map.93 = (f32[7,7,24]{2,1,0:T(8,128)}, f32[32,1536]{1,0:T(8,128)}, f32[32,128]{1,0:T(8,128)}, bf16[128,128]{1,0:T(8,128)(2,1)}, bf16[1536,128]{1,0:T(8,128)(2,1)}, /*index=5*/f32[8,8,24,128]{3,2,1,0:T(8,128)}) custom-call(bf16[24,24,24]{2,1,0:T(8,128)(2,1)} %bitcast.10, f32[7,7,1536]{2,1,0:T(8,128)} %k_hbm.1, bf16[1536,128]{1,0:T(8,128)(2,1)} %w_hbm.1, ...), custom_call_target="tpu_custom_call" | custom-call | flops 600000000 | bytes 4000000 | tf_op jit(solution)/shard_map/pallas_call | solution.py:620
  76.5 2.6 %shard_map.94 = (f32[7,7,24]{2,1,0:T(8,128)}, f32[32,1536]{1,0:T(8,128)}, f32[32,128]{1,0:T(8,128)}, f32[8,8,24,128]{3,2,1,0:T(8,128)}) custom-call(f32[7,7,24]{2,1,0:T(8,128)} %get-tuple-element.14.kg_ref, f32[32,1536]{1,0:T(8,128)} %get-tuple-element.15.left_ref, f32[32,128]{1,0:T(8,128)} %get-tuple-element.16.right_ref, ...), custom_call_target="tpu_custom_call" | custom-call | flops 60000000 | bytes 2500000 | tf_op jit(solution)/shard_map/pallas_call | solution.py:640

commit v2 on v1

--- a/solution.py
+++ b/solution.py
@@ -53,10 +53,10 @@
 def kernel(
     ny, nz, nx,
     x_hbm, k_hbm, w_hbm, gh_hbm, err_hbm, r_hbm,
-    kg_out, left_out, right_out, w_out, ls4, cor,
+    kg_out, left_out, right_out, w_out, ls4_out, cor_out,
     x_ref, k_ref, w_ref, err_ref, r_ref,
     ghp, ghs, ws, rs, wf, x2, xz, xp, xs, mk, kflat, kt, conv32, cvf, gr, gb, rh1, rh2, g32,
-    eg, gg, es, cs, gt, st, rz, ys, ll, chl, rp, kgt, rk, yk, lsn,
+    eg, gg, es, cs, gt, st, rz, ys, ll, chl, rp, kgt, rk, yk, lsn, ls4, cor, left,
     s_in,
     s_xz, r_xz, s_es, r_es, s_cs, r_cs, s_gt, r_gt, s_rz, r_rz, s_ys, r_ys, s_lx, r_lx, s_lz, r_lz,
     s_lk, r_lk, s_rp, r_rp, s_rk, r_rk, s_yk, r_yk, s_in2, r_in2, s_gx, r_gx, s_cx, r_cx, s_cc, r_cc,
@@ -117,6 +117,14 @@
     greet(sibling)
     loop(1, ny, lambda s: greet(at_y(lax.rem(y + s, ny))))
 
+    pl.semaphore_wait(barrier, (nz - 1) + (nx - 1) + (ny - 1) + 1)
+
+    in_gh = copy(gh_hbm, ghs.at[pl.ds(0, POS)], s_in2.at[0], r_in2.at[0], sibling)
+    in_r = copy(r_hbm, rs, s_in2.at[1], r_in2.at[1], sibling)
+    in_w = copy(w_hbm, ws, s_in2.at[2], r_in2.at[2], sibling)
+    for one in (in_r, in_gh, in_w):
+        one.start()
+
     x2[...] = jnp.zeros((3, LX, OWN), F32)
     load_x.wait()
     for i in range(SIDE):
@@ -137,8 +145,11 @@
         term = dot(picks[j].astype(F32).astype(BF16), x2[j].astype(BF16), NT)
         packed = term if packed is None else packed + term
     xz[z] = packed.astype(BF16)
-    ghp[POS:, :] = jnp.zeros((LP - POS, 128), BF16)
-    ghs[POS:, :] = jnp.zeros((LP - POS, 128), BF16)
+
+    def xz_copy(s):
+        return copy(xz.at[z], xz.at[z], s_xz.at[s], r_xz.at[s], at_z(zpeer(s)))
+
+    loop(1, nz, lambda s: xz_copy(s).start())
 
     load_r.wait()
     load_err.wait()
@@ -157,19 +168,69 @@
             for part in range(2):
                 eg[q // 2, q % 2, 2 * rg + part] = e[8 * rg : 8 * rg + 8, 128 * part : 128 * part + 128]
 
-    pl.semaphore_wait(barrier, (nz - 1) + (nx - 1) + (ny - 1) + 1)
-
     es_copy = copy(eg.at[:, 1 - k], es, s_es.at[0], r_es.at[0], sibling)
-    in_gh = copy(gh_hbm, ghs.at[pl.ds(0, POS)], s_in2.at[0], r_in2.at[0], sibling)
-    in_r = copy(r_hbm, rs, s_in2.at[1], r_in2.at[1], sibling)
-    in_w = copy(w_hbm, ws, s_in2.at[2], r_in2.at[2], sibling)
-
-    def xz_copy(s):
-        return copy(xz.at[z], xz.at[z], s_xz.at[s], r_xz.at[s], at_z(zpeer(s)))
-
-    loop(1, nz, lambda s: xz_copy(s).start())
-    for one in (in_r, in_gh, es_copy, in_w):
-        one.start()
+    es_copy.start()
+
+    ghp[POS:, :] = jnp.zeros((LP - POS, 128), BF16)
+    ghs[POS:, :] = jnp.zeros((LP - POS, 128), BF16)
+
+    load_gh.wait()
+    in_gh.wait_recv()
+    in_r.wait_recv()
+    sh, sl = split2(rs[...])
+    both = jnp.concatenate([ghp[...], ghs[...]], axis=1)
+    g = dot(
+        jnp.concatenate([rh, sh, rl, sl], axis=1), jnp.concatenate([both, both], axis=1), NT
+    )
+    for rg in range(4):
+        for j in range(5):
+            gg[rg // 2, (rg % 2) * 5 + j] = g[8 * rg : 8 * rg + 8, 128 * j : 128 * j + 128]
+
+    es_copy.wait_recv()
+
+    def chip_sum(xx):
+        cs[xx, 0, 0:8] = eg[xx, k] + es[xx]
+        cs[xx, 0, 8:18] = gg[k]
+
+    loop(0, nx, chip_sum)
+    cs[x, 1] = cs[x, 0]
+
+    def cs_copy(s):
+        xx = lax.rem(x + s, nx)
+        return copy(cs.at[xx, 0], cs.at[x, 1], s_cs.at[s], r_cs.at[s], at_x(xx))
+
+    loop(1, nx, lambda s: cs_copy(s).start())
+
+    load_w.wait()
+    in_w.wait_recv()
+    wf[:, :, :, :, 0:128] = w_ref[...].astype(F32).reshape(nz, nx, 2, OWN, 128)
+    wf[:, :, :, :, 128:256] = ws[...].astype(F32).reshape(nz, nx, 2, OWN, 128)
+
+    def grad_rows(xx):
+        rows = wf[:, xx, k].reshape(ch, 256).astype(BF16)
+        return dot(rows, jnp.concatenate([ghp[...], ghs[...]], axis=1), NT)
+
+    gb[0] = grad_rows(far_x).astype(BF16)
+    far_right = copy(
+        gb.at[0, pl.ds(0, half)], rh1.at[0], s_gx.at[0], r_gx.at[0], at_x(right_x)
+    )
+    far_left = copy(
+        gb.at[0, pl.ds(half, half)], rh1.at[1], s_gx.at[1], r_gx.at[1], at_x(left_x)
+    )
+    far_right.start()
+    far_left.start()
+    gr[0] = grad_rows(right_x)
+    gr[1] = grad_rows(left_x)
+    g32[...] = grad_rows(x)
+
+    loop(1, nx, lambda s: cs_copy(s).wait_recv())
+    total = cs[0, 1]
+    for q in range(1, nx):
+        total = total + cs[q, 1]
+    st[...] = total[0:8]
+    gt[k] = total[8:18]
+    gt_copy = copy(gt.at[k], gt.at[k], s_gt.at[0], r_gt.at[0], sibling)
+    gt_copy.start()
 
     load_k.wait()
     for a in range(7):
@@ -189,64 +250,6 @@
     xp[:, 0:128] = jnp.zeros((ch, 128), F32)
     xp[:, 128 + LP :] = jnp.zeros((ch, LX - 128 - LP), F32)
 
-    load_gh.wait()
-    in_gh.wait_recv()
-    in_r.wait_recv()
-    sh, sl = split2(rs[...])
-    both = jnp.concatenate([ghp[...], ghs[...]], axis=1)
-    g = dot(
-        jnp.concatenate([rh, sh, rl, sl], axis=1), jnp.concatenate([both, both], axis=1), NT
-    )
-    for rg in range(4):
-        for j in range(5):
-            gg[rg // 2, (rg % 2) * 5 + j] = g[8 * rg : 8 * rg + 8, 128 * j : 128 * j + 128]
-
-    es_copy.wait_recv()
-
-    def chip_sum(xx):
-        cs[xx, 0, 0:8] = eg[xx, k] + es[xx]
-        cs[xx, 0, 8:18] = gg[k]
-
-    loop(0, nx, chip_sum)
-    cs[x, 1] = cs[x, 0]
-
-    def cs_copy(s):
-        xx = lax.rem(x + s, nx)
-        return copy(cs.at[xx, 0], cs.at[x, 1], s_cs.at[s], r_cs.at[s], at_x(xx))
-
-    loop(1, nx, lambda s: cs_copy(s).start())
-
-    load_w.wait()
-    in_w.wait_recv()
-    wf[:, :, :, :, 0:128] = w_ref[...].astype(F32).reshape(nz, nx, 2, OWN, 128)
-    wf[:, :, :, :, 128:256] = ws[...].astype(F32).reshape(nz, nx, 2, OWN, 128)
-
-    def grad_rows(xx):
-        rows = wf[:, xx, k].reshape(ch, 256).astype(BF16)
-        return dot(rows, jnp.concatenate([ghp[...], ghs[...]], axis=1), NT)
-
-    gb[0] = grad_rows(far_x).astype(BF16)
-    far_right = copy(
-        gb.at[0, pl.ds(0, half)], rh1.at[0], s_gx.at[0], r_gx.at[0], at_x(right_x)
-    )
-    far_left = copy(
-        gb.at[0, pl.ds(half, half)], rh1.at[1], s_gx.at[1], r_gx.at[1], at_x(left_x)
-    )
-    far_right.start()
-    far_left.start()
-    gr[0] = grad_rows(right_x)
-    gr[1] = grad_rows(left_x)
-    g32[...] = grad_rows(x)
-
-    loop(1, nx, lambda s: cs_copy(s).wait_recv())
-    total = cs[0, 1]
-    for q in range(1, nx):
-        total = total + cs[q, 1]
-    st[...] = total[0:8]
-    gt[k] = total[8:18]
-    gt_copy = copy(gt.at[k], gt.at[k], s_gt.at[0], r_gt.at[0], sibling)
-    gt_copy.start()
-
     loop(1, nz, lambda s: xz_copy(s).wait_recv())
     lane_x = lax.broadcasted_iota(jnp.int32, (16, LX), 1)
     for zz in range(nz):
@@ -305,11 +308,11 @@
     conv_pad = cvf[x, k]
     if ch < 256:
         conv_pad = jnp.concatenate([conv_pad, jnp.zeros((256 - ch, LP), BF16)], axis=0)
-    left = dot(gsplit, conv_pad, NT)
-    left = left[0:32] + left[32:64]
+    conv_left = dot(gsplit, conv_pad, NT)
+    conv_left = conv_left[0:32] + conv_left[32:64]
     for rg in range(4):
         for part in range(2):
-            st[2 * rg + part] += left[8 * rg : 8 * rg + 8, 128 * part : 128 * part + 128]
+            st[2 * rg + part] += conv_left[8 * rg : 8 * rg + 8, 128 * part : 128 * part + 128]
 
     def rz_copy(s):
         zz = zpeer(s)
@@ -348,8 +351,6 @@
 
     if ch < 256:
         chl[:, ch:, :] = jnp.zeros((nxk, 256 - ch, 256), BF16)
-    local_grad(x, k)
-
     loop(1, ny, lambda s: ys_copy(s).wait_recv())
     total = ys[0]
     for q in range(1, ny):
@@ -362,6 +363,18 @@
 
     loop(1, nx, lambda s: lx_copy(s).start())
 
+    local_grad(x, k)
+    def lx_wait(s):
+        got = ll.at[k, z, lax.rem(x - s + nx, nx)]
+        copy(got, got, s_lx.at[s], r_lx.at[s], at_x(lax.rem(x + s, nx))).wait_recv()
+
+    loop(1, nx, lx_wait)
+
+    def lz_copy(s):
+        own = ll.at[k, z]
+        return copy(own, own, s_lz.at[s], r_lz.at[s], at_z(zpeer(s)))
+
+    loop(1, nz, lambda s: lz_copy(s).start())
     cx_copies[0].wait_recv()
     part0 = cvf.at[left_x, k, pl.ds(0, half)]
     cx_copies.append(copy(part0, part0, s_cx.at[2], r_cx.at[2], at_x(right_x)))
@@ -375,17 +388,6 @@
     local_grad(left_x, k)
     local_grad(right_x, k)
 
-    def lx_wait(s):
-        got = ll.at[k, z, lax.rem(x - s + nx, nx)]
-        copy(got, got, s_lx.at[s], r_lx.at[s], at_x(lax.rem(x + s, nx))).wait_recv()
-
-    loop(1, nx, lx_wait)
-
-    def lz_copy(s):
-        own = ll.at[k, z]
-        return copy(own, own, s_lz.at[s], r_lz.at[s], at_z(zpeer(s)))
-
-    loop(1, nz, lambda s: lz_copy(s).start())
     for s in range(3):
         cc_copy(s).wait_recv()
         local_grad(sources[s], 1 - k)
@@ -393,6 +395,10 @@
     def lz_wait(s):
         got = ll.at[k, lax.rem(z - s + nz, nz)]
         copy(got, got, s_lz.at[s], r_lz.at[s], at_z(zpeer(s))).wait_recv()
+
+    loop(1, nz, lz_wait)
+    lk_copy = copy(ll.at[k], ll.at[k], s_lk.at[0], r_lk.at[0], sibling)
+    lk_copy.start()
 
     near_right.wait_recv()
     near_left.wait_recv()
@@ -419,14 +425,15 @@
     loop(1, nz, lambda s: rk_copy(s).start())
     rk[z] = kgt[z]
 
-    loop(1, nz, lz_wait)
-    lk_copy = copy(ll.at[k], ll.at[k], s_lk.at[0], r_lk.at[0], sibling)
-    lk_copy.start()
 
     cx_copies[2].wait_recv()
     cx_copies[3].wait_recv()
     cc_copy(3).start()
     local_grad(far_x, k)
+    cc_copy(3).wait_recv()
+    local_grad(far_x, 1 - k)
+    cor_store = pltpu.make_async_copy(cor, cor_out, s_in.at[6])
+    cor_store.start()
     lk_copy.wait_recv()
 
     def left_of(q):
@@ -437,6 +444,18 @@
         return jnp.concatenate(rows, axis=0)
 
     lefts = [left_of(q) for q in range(nxk)]
+    right = None
+    for q in range(nxk):
+        term = dot(jnp.concatenate(split2(lefts[q]), axis=0), chl[q], NN)
+        right = term if q == 0 else right + term
+    right = right[0:32] + right[32:64]
+    rp[y] = right[:, 0:128] + right[:, 128:256]
+
+    def rp_copy(s):
+        return copy(rp.at[y], rp.at[y], s_rp.at[s], r_rp.at[s], at_y(lax.rem(y + s, ny)))
+
+    loop(1, ny, lambda s: rp_copy(s).start())
+
     wide3 = split3(jnp.concatenate(lefts, axis=1))
     stack3 = jnp.concatenate(wide3, axis=0)
     gram = None
@@ -449,6 +468,8 @@
     natural = lsn[...].reshape(channels, RANK).T
     nh, nm, nl = split3(natural)
     ls4[...] = jnp.concatenate([nh, nm, nh, nm], axis=0).T
+    ls4_store = pltpu.make_async_copy(ls4, ls4_out, s_in.at[7])
+    ls4_store.start()
 
     row_id = lax.broadcasted_iota(jnp.int32, (RANK, RANK), 0)
     lane_id = lax.broadcasted_iota(jnp.int32, (RANK, RANK), 1)
@@ -478,14 +499,13 @@
     scale = scale * (1.5 - 0.5 * diag * scale * scale)
     linv = aug[:, RANK:] * scale
     ih, im, il = split3(linv)
-    left_out[...] = dot(
+    left[...] = dot(
         jnp.concatenate([ih, ih, ih, im, im, il], axis=1),
         jnp.concatenate([nh, nm, nl, nh, nm, nh], axis=0),
         NN,
     )
-
-    cc_copy(3).wait_recv()
-    local_grad(far_x, 1 - k)
+    left_store = pltpu.make_async_copy(left, left_out, s_in.at[8])
+    left_store.start()
 
     loop(1, nz, lambda s: rk_copy(s).wait_recv())
     total = rk[0]
@@ -497,18 +517,6 @@
         return copy(yk.at[y], yk.at[y], s_yk.at[s], r_yk.at[s], at_y(lax.rem(y + s, ny)))
 
     loop(1, ny, lambda s: yk_copy(s).start())
-
-    right = None
-    for q in range(nxk):
-        term = dot(jnp.concatenate(split2(left_of(q)), axis=0), chl[q], NN)
-        right = term if q == 0 else right + term
-    right = right[0:32] + right[32:64]
-    rp[y] = right[:, 0:128] + right[:, 128:256]
-
-    def rp_copy(s):
-        return copy(rp.at[y], rp.at[y], s_rp.at[s], r_rp.at[s], at_y(lax.rem(y + s, ny)))
-
-    loop(1, ny, lambda s: rp_copy(s).start())
 
     loop(1, ny, lambda s: rp_copy(s).wait_recv())
     total = rp[0]
@@ -527,6 +535,8 @@
     for a in range(7):
         kg_out[a] = total[7 * a : 7 * a + 7]
 
+    for one in (cor_store, ls4_store, left_store):
+        one.wait()
     loop(1, nz, lambda s: xz_copy(s).wait_send())
     es_copy.wait_send()
     for one in (in_r, in_gh, in_w):
@@ -603,11 +613,15 @@
         vmem((nz, OWN, 128), F32),
         vmem((ny, OWN, 128), F32),
         vmem((nz, nxk, OWN, RANK), F32),
+        vmem((channels, 4 * RANK), BF16),
+        vmem((nz, nxk, OWN, 128), F32),
+        vmem((RANK, channels), F32),
     ]
-    sems = [pltpu.SemaphoreType.DMA((6,))]
+    sems = [pltpu.SemaphoreType.DMA((9,))]
     for count in (nz, 2, nx, 1, nz, ny, nx, nz, 1, ny, nz, ny, 4, 4, 4, 4):
         sems += [pltpu.SemaphoreType.DMA((count,))] * 2
     spec = pl.BlockSpec(memory_space=pltpu.VMEM)
+    far = pl.BlockSpec(memory_space=pl.ANY)
     cor_shape = jax.ShapeDtypeStruct((nz, nxk, OWN, 128), F32)
     mids = (
         jax.ShapeDtypeStruct((7, 7, OWN), F32),
@@ -621,7 +635,7 @@
         functools.partial(kernel, ny, nz, nx),
         out_shape=mids,
         in_specs=[pl.BlockSpec(memory_space=pl.ANY)] * 6,
-        out_specs=(spec,) * 6,
+        out_specs=(spec, far, spec, spec, far, far),
         scratch_shapes=scratch + sems,
         compiler_params=pltpu.CompilerParams(
             collective_id=0, has_side_effects=True, vmem_limit_bytes=60 * 1024 * 1024
@@ -637,11 +651,24 @@
         error_old.reshape(nz, nxk, OWN, 128),
         right_init.T,
     )
+    steps = min(4, nz)
+
+    def whole(shape):
+        return pl.BlockSpec(shape, lambda i: (0,) * len(shape))
+
+    rows = pl.BlockSpec((nz // steps, nxk, OWN, 128), lambda i: (i, 0, 0, 0))
+    small = [whole((7, 7, OWN)), whole((RANK, channels)), whole((RANK, 128))]
     kg, left, right, err = pl.pallas_call(
         finish,
+        grid=(steps,),
         out_shape=mids[0:3] + (cor_shape,),
-        in_specs=[spec] * 6,
-        out_specs=(spec,) * 4,
+        in_specs=small
+        + [
+            whole((4 * RANK, 128)),
+            pl.BlockSpec((channels // steps, 4 * RANK), lambda i: (i, 0)),
+            rows,
+        ],
+        out_specs=tuple(small) + (rows,),
         compiler_params=pltpu.CompilerParams(vmem_limit_bytes=60 * 1024 * 1024),
         cost_estimate=pl.CostEstimate(
             flops=60_000_000, bytes_accessed=2_500_000, transcendentals=0

time: 80.2 us -> 85.6 us (1.067); the launches traced: 79.1 us -> 85.4 us
  Pallas kernels: 78.5 us -> 84.7 us
    pallas_call x1, Pallas kernels: 75.9 us -> 80.9 us  [on_device(): pl.pallas_call(functools.partial(kernel, ny, nz, nx), out_shape=mids, in_...]
    pallas_call x1, Pallas kernels: 2.58 us -> 3.8 us  [on_device(): pl.pallas_call(finish, grid=(steps,), out_shape=mids[0:3] + (cor_shape,),...]
where the time goes in v2:
time: 85.6 us; the launch traced here: 85.4 us
  Pallas kernels  84.7 us (99%)
    pallas_call x1, Pallas kernels, on_device(): pl.pallas_call(functools.partial(kernel, ny, nz, nx), out_shape=mids, in_...  80.9 us
    pallas_call x1, Pallas kernels, on_device(): pl.pallas_call(finish, grid=(steps,), out_shape=mids[0:3] + (cor_shape,),...  3.8 us

profile of v2, /device:TPU:1, one launch (start us, length us, event | category | flops | bytes accessed | tf_op | source)
XLA Modules:
  0.0 85.4 jit_solution(9247220191431609301)
XLA Ops:
  0.6 80.9 %shard_map.93 = (f32[7,7,24]{2,1,0:T(8,128)}, f32[32,1536]{1,0:T(8,128)}, f32[32,128]{1,0:T(8,128)}, bf16[128,128]{1,0:T(8,128)(2,1)}, bf16[1536,128]{1,0:T(8,128)(2,1)}, /*index=5*/f32[8,8,24,128]{3,2,1,0:T(8,128)}) custom-call(bf16[24,24,24]{2,1,0:T(8,128)(2,1)} %bitcast.10, f32[7,7,1536]{2,1,0:T(8,128)} %k_hbm.1, bf16[1536,128]{1,0:T(8,128)(2,1)} %w_hbm.1, ...), custom_call_target="tpu_custom_call" | custom-call | flops 600000000 | bytes 4000000 | tf_op jit(solution)/shard_map/pallas_call | solution.py:634
  81.6 3.8 %shard_map.94 = (f32[7,7,24]{2,1,0:T(8,128)}, f32[32,1536]{1,0:T(8,128)}, f32[32,128]{1,0:T(8,128)}, f32[8,8,24,128]{3,2,1,0:T(8,128)}) custom-call(f32[7,7,24]{2,1,0:T(8,128)} %get-tuple-element.14.kg_ref, f32[32,1536]{1,0:T(8,128)} %get-tuple-element.15.left_ref, f32[32,128]{1,0:T(8,128)} %get-tuple-element.16.right_ref, ...), custom_call_target="tpu_custom_call" | custom-call | flops 60000000 | bytes 2500000 | tf_op jit(solution)/shard_map/pallas_call | solution.py:661

commit v3 on v2

--- a/solution.py
+++ b/solution.py
@@ -55,10 +55,10 @@
     x_hbm, k_hbm, w_hbm, gh_hbm, err_hbm, r_hbm,
     kg_out, left_out, right_out, w_out, ls4_out, cor_out,
     x_ref, k_ref, w_ref, err_ref, r_ref,
-    ghp, ghs, ws, rs, wf, x2, xz, xp, xs, mk, kflat, kt, conv32, cvf, gr, gb, rh1, rh2, g32,
+    ghp, ghs, ws, rs, wf, x2, xo, conv24, cz, xz, xp, mk, kflat, kt, conv32, cvf, gr, gb, rh1, rh2, g32,
     eg, gg, es, cs, gt, st, rz, ys, ll, chl, rp, kgt, rk, yk, lsn, ls4, cor, left,
     s_in,
-    s_xz, r_xz, s_es, r_es, s_cs, r_cs, s_gt, r_gt, s_rz, r_rz, s_ys, r_ys, s_lx, r_lx, s_lz, r_lz,
+    s_cz, r_cz, s_xz, r_xz, s_es, r_es, s_cs, r_cs, s_gt, r_gt, s_rz, r_rz, s_ys, r_ys, s_lx, r_lx, s_lz, r_lz,
     s_lk, r_lk, s_rp, r_rp, s_rk, r_rk, s_yk, r_yk, s_in2, r_in2, s_gx, r_gx, s_cx, r_cx, s_cc, r_cc,
 ):
     nxk = 2 * nx
@@ -125,26 +125,78 @@
     for one in (in_r, in_gh, in_w):
         one.start()
 
-    x2[...] = jnp.zeros((3, LX, OWN), F32)
+    x2[POS:, :] = jnp.zeros((LP - POS, OWN), F32)
     load_x.wait()
     for i in range(SIDE):
-        image_row = x_ref[i].astype(F32)
-        x2[0, SIDE * i : SIDE * (i + 1), :] = image_row
-        late = i >= SIDE // 2
-        at = POS + SIDE * (i % (SIDE // 2))
-        x2[2 if late else 1, at : at + SIDE, :] = image_row
-    out_row = lax.broadcasted_iota(jnp.int32, (16, OWN), 0)
-    channel = lax.broadcasted_iota(jnp.int32, (16, OWN), 1)
-    picks = (
-        channel == out_row,
-        (channel == out_row + 16) & (out_row < 8),
-        (channel == out_row + 8) & (out_row >= 8),
-    )
-    packed = None
-    for j in range(3):
-        term = dot(picks[j].astype(F32).astype(BF16), x2[j].astype(BF16), NT)
-        packed = term if packed is None else packed + term
-    xz[z] = packed.astype(BF16)
+        x2[SIDE * i : SIDE * (i + 1), :] = x_ref[i].astype(F32)
+    eye = (
+        lax.broadcasted_iota(jnp.int32, (32, OWN), 0)
+        == lax.broadcasted_iota(jnp.int32, (32, OWN), 1)
+    )
+    own = dot(eye.astype(F32).astype(BF16), x2[...].astype(BF16), NT)[0:OWN]
+    xo[:, 0:128] = jnp.zeros((OWN, 128), F32)
+    xo[:, 128 : 128 + LP] = own
+    xo[:, 128 + LP :] = jnp.zeros((OWN, LX - 128 - LP), F32)
+    load_k.wait()
+    for a in range(7):
+        kflat[8 * a : 8 * a + 7, :] = k_ref[a]
+        kflat[8 * a + 7 : 8 * a + 8, :] = jnp.zeros((1, channels), F32)
+    kflat[56:64, :] = jnp.zeros((8, channels), F32)
+    row = lax.broadcasted_iota(jnp.int32, (OWN, channels), 0)
+    lane = lax.broadcasted_iota(jnp.int32, (OWN, channels), 1)
+    pick = (lane - row == chip * OWN).astype(F32).astype(BF16)
+    three = jnp.concatenate(split3(kflat[...]), axis=0)
+    taps3 = dot(pick, three, NT)
+    kt[...] = taps3[:, 0:64] + taps3[:, 64:128] + taps3[:, 128:192]
+    pos = lax.broadcasted_iota(jnp.int32, (8, LP), 1)
+    col = lax.rem(pos, SIDE) + lax.broadcasted_iota(jnp.int32, (8, LP), 0) - 3
+    mk[...] = ((col >= 0) & (col < SIDE) & (pos < POS)).astype(F32)
+
+    def shifted(v):
+        return [pltpu.roll(v, LX - (96 + SIDE * (a - 3)), 1)[:, 0:LP] for a in range(7)]
+
+    for t in range(OWN // 8):
+        rows = slice(8 * t, 8 * t + 8)
+        taps = kt[rows, :]
+        moved = shifted(xo[rows, :])
+        out = None
+        for b in range(7):
+            part = None
+            for a in range(7):
+                term = taps[:, 8 * a + b : 8 * a + b + 1] * moved[a]
+                part = term if a == 0 else part + term
+            part = pltpu.roll(part, LP - (32 + b - 3), 1) * mk[b : b + 1, :]
+            out = part if b == 0 else out + part
+        conv24[rows, :] = out
+
+    lane_x = lax.broadcasted_iota(jnp.int32, (16, LX), 1)
+
+    def pack(v):
+        wide = jnp.concatenate([v, jnp.zeros((OWN, LX - LP), F32)], axis=1)
+        last = wide[16:24]
+        early = jnp.where(lane_x[0:8] < POS // 2, last, 0.0)
+        late = jnp.where(lane_x[0:8] < POS // 2, 0.0, last)
+        tail = jnp.concatenate(
+            [pltpu.roll(early, POS, 1), pltpu.roll(late, POS // 2, 1)], axis=0
+        )
+        return (wide[0:16] + tail).astype(BF16)
+
+    def unpack(v):
+        v = v.astype(F32)
+        early = pltpu.roll(v[0:8], LX - POS, 1)
+        late = pltpu.roll(v[8:16], LX - POS // 2, 1)
+        last = jnp.where(
+            lane_x[0:8] < POS // 2, early, jnp.where(lane_x[0:8] < POS, late, 0.0)
+        )
+        return jnp.where(lane_x < POS, v, 0.0)[:, 0:LP], last[:, 0:LP]
+
+    cz[z] = pack(conv24[...])
+
+    def cz_copy(s):
+        return copy(cz.at[z], cz.at[z], s_cz.at[s], r_cz.at[s], at_z(zpeer(s)))
+
+    loop(1, nz, lambda s: cz_copy(s).start())
+    xz[z] = pack(own)
 
     def xz_copy(s):
         return copy(xz.at[z], xz.at[z], s_xz.at[s], r_xz.at[s], at_z(zpeer(s)))
@@ -232,54 +284,11 @@
     gt_copy = copy(gt.at[k], gt.at[k], s_gt.at[0], r_gt.at[0], sibling)
     gt_copy.start()
 
-    load_k.wait()
-    for a in range(7):
-        kflat[8 * a : 8 * a + 7, :] = k_ref[a]
-        kflat[8 * a + 7 : 8 * a + 8, :] = jnp.zeros((1, channels), F32)
-    kflat[56:64, :] = jnp.zeros((8, channels), F32)
-    row = lax.broadcasted_iota(jnp.int32, (OWN, channels), 0)
-    lane = lax.broadcasted_iota(jnp.int32, (OWN, channels), 1)
-    apart = lane - row - xk * OWN
-    pick = jnp.concatenate([(apart == zz * nxk * OWN).astype(F32) for zz in range(nz)], axis=0)
-    three = jnp.concatenate(split3(kflat[...]), axis=0)
-    taps3 = dot(pick.astype(BF16), three, NT)
-    kt[...] = taps3[:, 0:64] + taps3[:, 64:128] + taps3[:, 128:192]
-    pos = lax.broadcasted_iota(jnp.int32, (8, LP), 1)
-    col = lax.rem(pos, SIDE) + lax.broadcasted_iota(jnp.int32, (8, LP), 0) - 3
-    mk[...] = ((col >= 0) & (col < SIDE) & (pos < POS)).astype(F32)
-    xp[:, 0:128] = jnp.zeros((ch, 128), F32)
-    xp[:, 128 + LP :] = jnp.zeros((ch, LX - 128 - LP), F32)
-
-    loop(1, nz, lambda s: xz_copy(s).wait_recv())
-    lane_x = lax.broadcasted_iota(jnp.int32, (16, LX), 1)
+    loop(1, nz, lambda s: cz_copy(s).wait_recv())
     for zz in range(nz):
-        v = xz[zz].astype(F32)
-        xp[OWN * zz : OWN * zz + 16, 128 : 128 + LP] = jnp.where(lane_x < POS, v, 0.0)[:, 0:LP]
-        early = pltpu.roll(v[0:8], LX - POS, 1)
-        late = pltpu.roll(v[8:16], LX - POS // 2, 1)
-        last = jnp.where(
-            lane_x[0:8] < POS // 2, early, jnp.where(lane_x[0:8] < POS, late, 0.0)
-        )
-        xp[OWN * zz + 16 : OWN * zz + 24, 128 : 128 + LP] = last[:, 0:LP]
-
-    def conv_rows(t):
-        rows = pl.ds(pl.multiple_of(t * 8, 8), 8)
-        v = xp[rows, :]
-        taps = kt[rows, :]
-        moved = [pltpu.roll(v, LX - (96 + SIDE * (a - 3)), 1)[:, 0:LP] for a in range(7)]
-        for a in range(7):
-            xs[a, rows, :] = moved[a]
-        out = None
-        for b in range(7):
-            part = None
-            for a in range(7):
-                term = taps[:, 8 * a + b : 8 * a + b + 1] * moved[a]
-                part = term if a == 0 else part + term
-            part = pltpu.roll(part, LP - (32 + b - 3), 1) * mk[b : b + 1, :]
-            out = part if b == 0 else out + part
-        conv32[rows, :] = out
-
-    loop(0, ch // 8, conv_rows, 2)
+        first, last = unpack(cz[zz])
+        conv32[OWN * zz : OWN * zz + 16, :] = first
+        conv32[OWN * zz + 16 : OWN * zz + 24, :] = last
     cvf[x, k] = conv32[...].astype(BF16)
 
     mine = cvf.at[x, k]
@@ -400,40 +409,50 @@
     lk_copy = copy(ll.at[k], ll.at[k], s_lk.at[0], r_lk.at[0], sibling)
     lk_copy.start()
 
-    near_right.wait_recv()
-    near_left.wait_recv()
-    g32[...] += rh2[0].astype(F32) + rh2[1].astype(F32)
-    lane128 = lax.broadcasted_iota(jnp.int32, (8, 128), 1)
-
-    def kernel_terms(t):
-        rows = pl.ds(pl.multiple_of(t * 8, 8), 8)
-        gt = g32[rows, :]
-        out = jnp.zeros((8, 128), F32)
-        for b in range(7):
-            gm = pltpu.roll(gt * mk[b : b + 1, :], 32 + b - 3, 1)
-            for a in range(7):
-                one = jnp.sum(gm * xs[a, rows, :], axis=1, keepdims=True)
-                out = jnp.where(lane128 == 7 * a + b, one, out)
-        kgt[t // 3, pl.ds(pl.multiple_of(lax.rem(t, 3) * 8, 8), 8), :] = out
-
-    loop(0, ch // 8, kernel_terms, 2)
-
-    def rk_copy(s):
-        zz = zpeer(s)
-        return copy(kgt.at[zz], rk.at[z], s_rk.at[s], r_rk.at[s], at_z(zz))
-
-    loop(1, nz, lambda s: rk_copy(s).start())
-    rk[z] = kgt[z]
-
-
     cx_copies[2].wait_recv()
     cx_copies[3].wait_recv()
     cc_copy(3).start()
     local_grad(far_x, k)
-    cc_copy(3).wait_recv()
-    local_grad(far_x, 1 - k)
-    cor_store = pltpu.make_async_copy(cor, cor_out, s_in.at[6])
-    cor_store.start()
+
+    loop(1, nz, lambda s: xz_copy(s).wait_recv())
+    xp[:, 0:128] = jnp.zeros((ch, 128), F32)
+    xp[:, 128 + LP :] = jnp.zeros((ch, LX - 128 - LP), F32)
+    for zz in range(nz):
+        first, last = unpack(xz[zz])
+        xp[OWN * zz : OWN * zz + 16, 128 : 128 + LP] = first
+        xp[OWN * zz + 16 : OWN * zz + 24, 128 : 128 + LP] = last
+    near_right.wait_recv()
+    near_left.wait_recv()
+    g32[...] += rh2[0].astype(F32) + rh2[1].astype(F32)
+    pair_row = lax.broadcasted_iota(jnp.int32, (OWN, 7 * OWN), 0)
+    pair_lane = lax.broadcasted_iota(jnp.int32, (OWN, 7 * OWN), 1)
+    diagonal = lax.rem(pair_lane, OWN) == pair_row
+    tap_row = lax.broadcasted_iota(jnp.int32, (8, 7 * OWN), 0)
+
+    def kernel_terms(zz):
+        rows = pl.ds(pl.multiple_of(zz * OWN, 8), OWN)
+        maps = jnp.concatenate(shifted(xp[rows, :]), axis=0).astype(BF16)
+        gt = g32[rows, :]
+        moved = [pltpu.roll(gt * mk[b : b + 1, :], 32 + b - 3, 1) for b in range(7)]
+        hi, lo = split2(jnp.concatenate(moved, axis=0))
+        pairs = dot(hi, maps, NT) + dot(lo, maps, NT)
+        out = jnp.zeros((8, 7 * OWN), F32)
+        for b in range(7):
+            block = jnp.where(diagonal, pairs[OWN * b : OWN * (b + 1)], 0.0)
+            one = jnp.sum(block, axis=0, keepdims=True)
+            out = jnp.where(tap_row == b, one, out)
+        kgt[zz] = jnp.concatenate([out, jnp.zeros((8, 256 - 7 * OWN), F32)], axis=1)
+
+    loop(0, nz, kernel_terms, 2)
+
+    def rk_copy(s):
+        zz = zpeer(s)
+        return copy(kgt.at[zz], rk.at[z], s_rk.at[s], r_rk.at[s], at_z(zz))
+
+    loop(1, nz, lambda s: rk_copy(s).start())
+    rk[z] = kgt[z]
+
+
     lk_copy.wait_recv()
 
     def left_of(q):
@@ -444,18 +463,6 @@
         return jnp.concatenate(rows, axis=0)
 
     lefts = [left_of(q) for q in range(nxk)]
-    right = None
-    for q in range(nxk):
-        term = dot(jnp.concatenate(split2(lefts[q]), axis=0), chl[q], NN)
-        right = term if q == 0 else right + term
-    right = right[0:32] + right[32:64]
-    rp[y] = right[:, 0:128] + right[:, 128:256]
-
-    def rp_copy(s):
-        return copy(rp.at[y], rp.at[y], s_rp.at[s], r_rp.at[s], at_y(lax.rem(y + s, ny)))
-
-    loop(1, ny, lambda s: rp_copy(s).start())
-
     wide3 = split3(jnp.concatenate(lefts, axis=1))
     stack3 = jnp.concatenate(wide3, axis=0)
     gram = None
@@ -470,6 +477,23 @@
     ls4[...] = jnp.concatenate([nh, nm, nh, nm], axis=0).T
     ls4_store = pltpu.make_async_copy(ls4, ls4_out, s_in.at[7])
     ls4_store.start()
+
+    cc_copy(3).wait_recv()
+    local_grad(far_x, 1 - k)
+    cor_store = pltpu.make_async_copy(cor, cor_out, s_in.at[6])
+    cor_store.start()
+
+    right = None
+    for q in range(nxk):
+        term = dot(jnp.concatenate(split2(lefts[q]), axis=0), chl[q], NN)
+        right = term if q == 0 else right + term
+    right = right[0:32] + right[32:64]
+    rp[y] = right[:, 0:128] + right[:, 128:256]
+
+    def rp_copy(s):
+        return copy(rp.at[y], rp.at[y], s_rp.at[s], r_rp.at[s], at_y(lax.rem(y + s, ny)))
+
+    loop(1, ny, lambda s: rp_copy(s).start())
 
     row_id = lax.broadcasted_iota(jnp.int32, (RANK, RANK), 0)
     lane_id = lax.broadcasted_iota(jnp.int32, (RANK, RANK), 1)
@@ -531,12 +555,12 @@
     total = yk[0]
     for q in range(1, ny):
         total = total + yk[q]
-    total = total.T
     for a in range(7):
-        kg_out[a] = total[7 * a : 7 * a + 7]
+        kg_out[a] = total[0:7, OWN * a : OWN * (a + 1)]
 
     for one in (cor_store, ls4_store, left_store):
         one.wait()
+    loop(1, nz, lambda s: cz_copy(s).wait_send())
     loop(1, nz, lambda s: xz_copy(s).wait_send())
     es_copy.wait_send()
     for one in (in_r, in_gh, in_w):
@@ -584,13 +608,15 @@
         vmem((channels, 128), BF16),
         vmem((RANK, 128), F32),
         vmem((nz, nx, 2, OWN, 256), F32),
-        vmem((3, LX, OWN), F32),
+        vmem((LP, OWN), F32),
+        vmem((OWN, LX), F32),
+        vmem((OWN, LP), F32),
+        vmem((nz, 16, LX), BF16),
         vmem((nz, 16, LX), BF16),
         vmem((ch, LX), F32),
-        vmem((7, ch, LP), F32),
         vmem((8, LP), F32),
         vmem((64, channels), F32),
-        vmem((ch, 64), F32),
+        vmem((OWN, 64), F32),
         vmem((ch, LP), F32),
         vmem((nx, 2, ch, LP), BF16),
         vmem((2, ch, LP), F32),
@@ -609,16 +635,16 @@
         vmem((2, nz, nx, tpz, 8, 128), F32),
         vmem((nxk, 256, 256), BF16),
         vmem((ny, RANK, 128), F32),
-        vmem((nz, OWN, 128), F32),
-        vmem((nz, OWN, 128), F32),
-        vmem((ny, OWN, 128), F32),
+        vmem((nz, 8, 256), F32),
+        vmem((nz, 8, 256), F32),
+        vmem((ny, 8, 256), F32),
         vmem((nz, nxk, OWN, RANK), F32),
         vmem((channels, 4 * RANK), BF16),
         vmem((nz, nxk, OWN, 128), F32),
         vmem((RANK, channels), F32),
     ]
     sems = [pltpu.SemaphoreType.DMA((9,))]
-    for count in (nz, 2, nx, 1, nz, ny, nx, nz, 1, ny, nz, ny, 4, 4, 4, 4):
+    for count in (nz, nz, 2, nx, 1, nz, ny, nx, nz, 1, ny, nz, ny, 4, 4, 4, 4):
         sems += [pltpu.SemaphoreType.DMA((count,))] * 2
     spec = pl.BlockSpec(memory_space=pltpu.VMEM)
     far = pl.BlockSpec(memory_space=pl.ANY)
@@ -651,24 +677,11 @@
         error_old.reshape(nz, nxk, OWN, 128),
         right_init.T,
     )
-    steps = min(4, nz)
-
-    def whole(shape):
-        return pl.BlockSpec(shape, lambda i: (0,) * len(shape))
-
-    rows = pl.BlockSpec((nz // steps, nxk, OWN, 128), lambda i: (i, 0, 0, 0))
-    small = [whole((7, 7, OWN)), whole((RANK, channels)), whole((RANK, 128))]
     kg, left, right, err = pl.pallas_call(
         finish,
-        grid=(steps,),
         out_shape=mids[0:3] + (cor_shape,),
-        in_specs=small
-        + [
-            whole((4 * RANK, 128)),
-            pl.BlockSpec((channels // steps, 4 * RANK), lambda i: (i, 0)),
-            rows,
-        ],
-        out_specs=tuple(small) + (rows,),
+        in_specs=[spec] * 6,
+        out_specs=(spec,) * 4,
         compiler_params=pltpu.CompilerParams(vmem_limit_bytes=60 * 1024 * 1024),
         cost_estimate=pl.CostEstimate(
             flops=60_000_000, bytes_accessed=2_500_000, transcendentals=0

time: 85.6 us -> 62.1 us (0.73)
  the two profiles are of different devices: /device:TPU:1 before, /device:TPU:2 now
where the time goes in v3:
time: 62.1 us; the launch traced here: 61.9 us
  Pallas kernels  61.3 us (99%)
  between operations  0.64 us (1%)
    pallas_call x1, Pallas kernels, on_device(): pl.pallas_call(functools.partial(kernel, ny, nz, nx), out_shape=mids, in_...  58.7 us
    pallas_call x1, Pallas kernels, on_device(): pl.pallas_call(finish, out_shape=mids[0:3] + (cor_shape,), in_specs=[spec...  2.58 us

profile of v3, /device:TPU:2, one launch (start us, length us, event | category | flops | bytes accessed | tf_op | source)
XLA Modules:
  0.0 61.9 jit_solution(460293704977481027)
XLA Ops:
  0.6 58.7 %shard_map.93 = (f32[7,7,24]{2,1,0:T(8,128)}, f32[32,1536]{1,0:T(8,128)}, f32[32,128]{1,0:T(8,128)}, bf16[128,128]{1,0:T(8,128)(2,1)}, bf16[1536,128]{1,0:T(8,128)(2,1)}, /*index=5*/f32[8,8,24,128]{3,2,1,0:T(8,128)}) custom-call(bf16[24,24,24]{2,1,0:T(8,128)(2,1)} %bitcast.10, f32[7,7,1536]{2,1,0:T(8,128)} %k_hbm.1, bf16[1536,128]{1,0:T(8,128)(2,1)} %w_hbm.1, ...), custom_call_target="tpu_custom_call" | custom-call | flops 600000000 | bytes 4000000 | tf_op jit(solution)/shard_map/pallas_call | solution.py:660
  59.3 2.6 %shard_map.94 = (f32[7,7,24]{2,1,0:T(8,128)}, f32[32,1536]{1,0:T(8,128)}, f32[32,128]{1,0:T(8,128)}, f32[8,8,24,128]{3,2,1,0:T(8,128)}) custom-call(f32[7,7,24]{2,1,0:T(8,128)} %get-tuple-element.14.kg_ref, f32[32,1536]{1,0:T(8,128)} %get-tuple-element.15.left_ref, f32[32,128]{1,0:T(8,128)} %get-tuple-element.16.right_ref, ...), custom_call_target="tpu_custom_call" | custom-call | flops 60000000 | bytes 2500000 | tf_op jit(solution)/shard_map/pallas_call | solution.py:680

commit v4 on v3

--- a/solution.py
+++ b/solution.py
@@ -201,7 +201,6 @@
     def xz_copy(s):
         return copy(xz.at[z], xz.at[z], s_xz.at[s], r_xz.at[s], at_z(zpeer(s)))
 
-    loop(1, nz, lambda s: xz_copy(s).start())
 
     load_r.wait()
     load_err.wait()
@@ -290,22 +289,6 @@
         conv32[OWN * zz : OWN * zz + 16, :] = first
         conv32[OWN * zz + 16 : OWN * zz + 24, :] = last
     cvf[x, k] = conv32[...].astype(BF16)
-
-    mine = cvf.at[x, k]
-    cx_copies = [
-        copy(mine, mine, s_cx.at[0], r_cx.at[0], at_x(right_x)),
-        copy(mine, mine, s_cx.at[1], r_cx.at[1], at_x(left_x)),
-    ]
-    for s in range(2):
-        cx_copies[s].start()
-
-    sources = (x, left_x, right_x, far_x)
-
-    def cc_copy(s):
-        block = cvf.at[sources[s], k]
-        return copy(block, block, s_cc.at[s], r_cc.at[s], sibling)
-
-    cc_copy(0).start()
 
     gt_copy.wait_recv()
     groups = []
@@ -329,6 +312,7 @@
 
     loop(1, nz, lambda s: rz_copy(s).start())
     rz[z] = st[pl.ds(z * tpz, tpz)]
+    loop(1, nz, lambda s: xz_copy(s).start())
 
     far_right.wait_recv()
     gb[1, 0:half, :] = (gr[0, 0:half, :] + rh1[0].astype(F32)).astype(BF16)
@@ -341,6 +325,22 @@
     near_left = copy(gb.at[2], rh2.at[1], s_gx.at[3], r_gx.at[3], at_x(left_x))
     near_left.start()
 
+    mine = cvf.at[x, k]
+    cx_copies = [
+        copy(mine, mine, s_cx.at[0], r_cx.at[0], at_x(right_x)),
+        copy(mine, mine, s_cx.at[1], r_cx.at[1], at_x(left_x)),
+    ]
+    for s in range(2):
+        cx_copies[s].start()
+
+    sources = (x, left_x, right_x, far_x)
+
+    def cc_copy(s):
+        block = cvf.at[sources[s], k]
+        return copy(block, block, s_cc.at[s], r_cc.at[s], sibling)
+
+    cc_copy(0).start()
+
     loop(1, nz, lambda s: rz_copy(s).wait_recv())
     total = rz[0]
     for q in range(1, nz):
@@ -373,46 +373,6 @@
     loop(1, nx, lambda s: lx_copy(s).start())
 
     local_grad(x, k)
-    def lx_wait(s):
-        got = ll.at[k, z, lax.rem(x - s + nx, nx)]
-        copy(got, got, s_lx.at[s], r_lx.at[s], at_x(lax.rem(x + s, nx))).wait_recv()
-
-    loop(1, nx, lx_wait)
-
-    def lz_copy(s):
-        own = ll.at[k, z]
-        return copy(own, own, s_lz.at[s], r_lz.at[s], at_z(zpeer(s)))
-
-    loop(1, nz, lambda s: lz_copy(s).start())
-    cx_copies[0].wait_recv()
-    part0 = cvf.at[left_x, k, pl.ds(0, half)]
-    cx_copies.append(copy(part0, part0, s_cx.at[2], r_cx.at[2], at_x(right_x)))
-    cx_copies[2].start()
-    cc_copy(1).start()
-    cx_copies[1].wait_recv()
-    part1 = cvf.at[right_x, k, pl.ds(half, half)]
-    cx_copies.append(copy(part1, part1, s_cx.at[3], r_cx.at[3], at_x(left_x)))
-    cx_copies[3].start()
-    cc_copy(2).start()
-    local_grad(left_x, k)
-    local_grad(right_x, k)
-
-    for s in range(3):
-        cc_copy(s).wait_recv()
-        local_grad(sources[s], 1 - k)
-
-    def lz_wait(s):
-        got = ll.at[k, lax.rem(z - s + nz, nz)]
-        copy(got, got, s_lz.at[s], r_lz.at[s], at_z(zpeer(s))).wait_recv()
-
-    loop(1, nz, lz_wait)
-    lk_copy = copy(ll.at[k], ll.at[k], s_lk.at[0], r_lk.at[0], sibling)
-    lk_copy.start()
-
-    cx_copies[2].wait_recv()
-    cx_copies[3].wait_recv()
-    cc_copy(3).start()
-    local_grad(far_x, k)
 
     loop(1, nz, lambda s: xz_copy(s).wait_recv())
     xp[:, 0:128] = jnp.zeros((ch, 128), F32)
@@ -452,6 +412,58 @@
     loop(1, nz, lambda s: rk_copy(s).start())
     rk[z] = kgt[z]
 
+    def lx_wait(s):
+        got = ll.at[k, z, lax.rem(x - s + nx, nx)]
+        copy(got, got, s_lx.at[s], r_lx.at[s], at_x(lax.rem(x + s, nx))).wait_recv()
+
+    loop(1, nx, lx_wait)
+
+    def lz_copy(s):
+        own = ll.at[k, z]
+        return copy(own, own, s_lz.at[s], r_lz.at[s], at_z(zpeer(s)))
+
+    loop(1, nz, lambda s: lz_copy(s).start())
+
+    cx_copies[0].wait_recv()
+    part0 = cvf.at[left_x, k, pl.ds(0, half)]
+    cx_copies.append(copy(part0, part0, s_cx.at[2], r_cx.at[2], at_x(right_x)))
+    cx_copies[2].start()
+    cc_copy(1).start()
+    cx_copies[1].wait_recv()
+    part1 = cvf.at[right_x, k, pl.ds(half, half)]
+    cx_copies.append(copy(part1, part1, s_cx.at[3], r_cx.at[3], at_x(left_x)))
+    cx_copies[3].start()
+    cc_copy(2).start()
+    local_grad(left_x, k)
+    local_grad(right_x, k)
+
+    for s in range(3):
+        cc_copy(s).wait_recv()
+        local_grad(sources[s], 1 - k)
+
+    loop(1, nz, lambda s: rk_copy(s).wait_recv())
+    total = rk[0]
+    for q in range(1, nz):
+        total = total + rk[q]
+    yk[y] = total
+
+    def yk_copy(s):
+        return copy(yk.at[y], yk.at[y], s_yk.at[s], r_yk.at[s], at_y(lax.rem(y + s, ny)))
+
+    loop(1, ny, lambda s: yk_copy(s).start())
+
+    def lz_wait(s):
+        got = ll.at[k, lax.rem(z - s + nz, nz)]
+        copy(got, got, s_lz.at[s], r_lz.at[s], at_z(zpeer(s))).wait_recv()
+
+    loop(1, nz, lz_wait)
+    lk_copy = copy(ll.at[k], ll.at[k], s_lk.at[0], r_lk.at[0], sibling)
+    lk_copy.start()
+
+    cx_copies[2].wait_recv()
+    cx_copies[3].wait_recv()
+    cc_copy(3).start()
+    local_grad(far_x, k)
 
     lk_copy.wait_recv()
 
@@ -530,17 +542,6 @@
     )
     left_store = pltpu.make_async_copy(left, left_out, s_in.at[8])
     left_store.start()
-
-    loop(1, nz, lambda s: rk_copy(s).wait_recv())
-    total = rk[0]
-    for q in range(1, nz):
-        total = total + rk[q]
-    yk[y] = total
-
-    def yk_copy(s):
-        return copy(yk.at[y], yk.at[y], s_yk.at[s], r_yk.at[s], at_y(lax.rem(y + s, ny)))
-
-    loop(1, ny, lambda s: yk_copy(s).start())
 
     loop(1, ny, lambda s: rp_copy(s).wait_recv())
     total = rp[0]

time: 62.1 us -> 60.4 us (0.973)
  the two profiles are of different devices: /device:TPU:2 before, /device:TPU:1 now
where the time goes in v4:
time: 60.4 us; the launch traced here: 60.2 us
  Pallas kernels  59.6 us (99%)
  between operations  0.64 us (1%)
    pallas_call x1, Pallas kernels, on_device(): pl.pallas_call(functools.partial(kernel, ny, nz, nx), out_shape=mids, in_...  57 us
    pallas_call x1, Pallas kernels, on_device(): pl.pallas_call(finish, out_shape=mids[0:3] + (cor_shape,), in_specs=[spec...  2.57 us

profile of v4, /device:TPU:1, one launch (start us, length us, event | category | flops | bytes accessed | tf_op | source)
XLA Modules:
  0.0 60.2 jit_solution(6897059772703961087)
XLA Ops:
  0.6 57.0 %shard_map.93 = (f32[7,7,24]{2,1,0:T(8,128)}, f32[32,1536]{1,0:T(8,128)}, f32[32,128]{1,0:T(8,128)}, bf16[128,128]{1,0:T(8,128)(2,1)}, bf16[1536,128]{1,0:T(8,128)(2,1)}, /*index=5*/f32[8,8,24,128]{3,2,1,0:T(8,128)}) custom-call(bf16[24,24,24]{2,1,0:T(8,128)(2,1)} %bitcast.10, f32[7,7,1536]{2,1,0:T(8,128)} %k_hbm.1, bf16[1536,128]{1,0:T(8,128)(2,1)} %w_hbm.1, ...), custom_call_target="tpu_custom_call" | custom-call | flops 600000000 | bytes 4000000 | tf_op jit(solution)/shard_map/pallas_call | solution.py:661
  57.7 2.6 %shard_map.94 = (f32[7,7,24]{2,1,0:T(8,128)}, f32[32,1536]{1,0:T(8,128)}, f32[32,128]{1,0:T(8,128)}, f32[8,8,24,128]{3,2,1,0:T(8,128)}) custom-call(f32[7,7,24]{2,1,0:T(8,128)} %get-tuple-element.14.kg_ref, f32[32,1536]{1,0:T(8,128)} %get-tuple-element.15.left_ref, f32[32,128]{1,0:T(8,128)} %get-tuple-element.16.right_ref, ...), custom_call_target="tpu_custom_call" | custom-call | flops 60000000 | bytes 2500000 | tf_op jit(solution)/shard_map/pallas_call | solution.py:681

commit v5 on v4

--- a/solution.py
+++ b/solution.py
@@ -117,14 +117,6 @@
     greet(sibling)
     loop(1, ny, lambda s: greet(at_y(lax.rem(y + s, ny))))
 
-    pl.semaphore_wait(barrier, (nz - 1) + (nx - 1) + (ny - 1) + 1)
-
-    in_gh = copy(gh_hbm, ghs.at[pl.ds(0, POS)], s_in2.at[0], r_in2.at[0], sibling)
-    in_r = copy(r_hbm, rs, s_in2.at[1], r_in2.at[1], sibling)
-    in_w = copy(w_hbm, ws, s_in2.at[2], r_in2.at[2], sibling)
-    for one in (in_r, in_gh, in_w):
-        one.start()
-
     x2[POS:, :] = jnp.zeros((LP - POS, OWN), F32)
     load_x.wait()
     for i in range(SIDE):
@@ -195,8 +187,18 @@
     def cz_copy(s):
         return copy(cz.at[z], cz.at[z], s_cz.at[s], r_cz.at[s], at_z(zpeer(s)))
 
+    xz[z] = pack(own)
+
+    pl.semaphore_wait(barrier, (nz - 1) + (nx - 1) + (ny - 1) + 1)
+
     loop(1, nz, lambda s: cz_copy(s).start())
-    xz[z] = pack(own)
+
+    in_gh = copy(gh_hbm, ghs.at[pl.ds(0, POS)], s_in2.at[0], r_in2.at[0], sibling)
+    in_r = copy(r_hbm, rs, s_in2.at[1], r_in2.at[1], sibling)
+    in_w = copy(w_hbm, ws, s_in2.at[2], r_in2.at[2], sibling)
+    for one in (in_r, in_gh, in_w):
+        one.start()
+
 
     def xz_copy(s):
         return copy(xz.at[z], xz.at[z], s_xz.at[s], r_xz.at[s], at_z(zpeer(s)))
@@ -543,13 +545,18 @@
     left_store = pltpu.make_async_copy(left, left_out, s_in.at[8])
     left_store.start()
 
+    inverse = dot(linv.T, linv, NN, HIGH) * (1.0 / workers)
+    ah, am, al = split3(jnp.concatenate([linv, inverse], axis=0))
+    final_left = jnp.concatenate([ah, ah, ah, am, am, al], axis=1)
+
     loop(1, ny, lambda s: rp_copy(s).wait_recv())
     total = rp[0]
     for q in range(1, ny):
         total = total + rp[q]
-    fright = dot(linv, total, NN, HIGH)
-    right_out[...] = fright
-    wh, wl = split2(dot(linv.T, fright, NN, HIGH) * (1.0 / workers))
+    th, tm, tl = split3(total)
+    solved = dot(final_left, jnp.concatenate([th, tm, tl, th, tm, th], axis=0), NN)
+    right_out[...] = solved[0:RANK]
+    wh, wl = split2(solved[RANK:])
     w_out[...] = jnp.concatenate([wh, wh, wl, wl], axis=0)
 
     loop(1, ny, lambda s: yk_copy(s).wait_recv())

time: 60.4 us -> 59.4 us (0.983)
  Pallas kernels: 59.6 us -> 58.6 us
    pallas_call x1, Pallas kernels: 57 us -> 56 us  [on_device(): pl.pallas_call(functools.partial(kernel, ny, nz, nx), out_shape=mids, in_...]
where the time goes in v5:
time: 59.4 us; the launch traced here: 59.2 us
  Pallas kernels  58.6 us (99%)
  between operations  0.64 us (1%)
    pallas_call x1, Pallas kernels, on_device(): pl.pallas_call(functools.partial(kernel, ny, nz, nx), out_shape=mids, in_...  56 us
    pallas_call x1, Pallas kernels, on_device(): pl.pallas_call(finish, out_shape=mids[0:3] + (cor_shape,), in_specs=[spec...  2.57 us

profile of v5, /device:TPU:1, one launch (start us, length us, event | category | flops | bytes accessed | tf_op | source)
XLA Modules:
  0.0 59.2 jit_solution(7344613593149342169)
XLA Ops:
  0.6 56.0 %shard_map.93 = (f32[7,7,24]{2,1,0:T(8,128)}, f32[32,1536]{1,0:T(8,128)}, f32[32,128]{1,0:T(8,128)}, bf16[128,128]{1,0:T(8,128)(2,1)}, bf16[1536,128]{1,0:T(8,128)(2,1)}, /*index=5*/f32[8,8,24,128]{3,2,1,0:T(8,128)}) custom-call(bf16[24,24,24]{2,1,0:T(8,128)(2,1)} %bitcast.10, f32[7,7,1536]{2,1,0:T(8,128)} %k_hbm.1, bf16[1536,128]{1,0:T(8,128)(2,1)} %w_hbm.1, ...), custom_call_target="tpu_custom_call" | custom-call | flops 600000000 | bytes 4000000 | tf_op jit(solution)/shard_map/pallas_call | solution.py:668
  56.7 2.6 %shard_map.94 = (f32[7,7,24]{2,1,0:T(8,128)}, f32[32,1536]{1,0:T(8,128)}, f32[32,128]{1,0:T(8,128)}, f32[8,8,24,128]{3,2,1,0:T(8,128)}) custom-call(f32[7,7,24]{2,1,0:T(8,128)} %get-tuple-element.14.kg_ref, f32[32,1536]{1,0:T(8,128)} %get-tuple-element.15.left_ref, f32[32,128]{1,0:T(8,128)} %get-tuple-element.16.right_ref, ...), custom_call_target="tpu_custom_call" | custom-call | flops 60000000 | bytes 2500000 | tf_op jit(solution)/shard_map/pallas_call | solution.py:688

commit v6 on v5

--- a/solution.py
+++ b/solution.py
@@ -55,7 +55,7 @@
     x_hbm, k_hbm, w_hbm, gh_hbm, err_hbm, r_hbm,
     kg_out, left_out, right_out, w_out, ls4_out, cor_out,
     x_ref, k_ref, w_ref, err_ref, r_ref,
-    ghp, ghs, ws, rs, wf, x2, xo, conv24, cz, xz, xp, mk, kflat, kt, conv32, cvf, gr, gb, rh1, rh2, g32,
+    ghp, ghs, ght, ws, rs, wf, x2, xo, conv24, cz, xz, xp, mk, kflat, kt, cvf, gr, gb, rh1, rh2, g32,
     eg, gg, es, cs, gt, st, rz, ys, ll, chl, rp, kgt, rk, yk, lsn, ls4, cor, left,
     s_in,
     s_cz, r_cz, s_xz, r_xz, s_es, r_es, s_cs, r_cs, s_gt, r_gt, s_rz, r_rz, s_ys, r_ys, s_lx, r_lx, s_lz, r_lz,
@@ -66,6 +66,7 @@
     channels = ch * nxk
     tpz = 8 // nz
     half = ch // 2
+    top = 16 * nz
     workers = ny
     y = lax.axis_index("outer")
     chip = lax.axis_index("chip")
@@ -96,6 +97,16 @@
         return pltpu.make_async_remote_copy(
             src_ref=src, dst_ref=dst, send_sem=ssem, recv_sem=rsem,
             device_id=dev, device_id_type=MESH,
+        )
+
+    def slots(v):
+        return jnp.concatenate(
+            [v[:, 0:16].reshape(top, v.shape[2]), v[:, 16:24].reshape(ch - top, v.shape[2])], axis=0
+        )
+
+    def natural_rows(v):
+        return jnp.concatenate(
+            [v[0:top].reshape(nz, 16, v.shape[1]), v[top:ch].reshape(nz, 8, v.shape[1])], axis=1
         )
 
     load_x = pltpu.make_async_copy(x_hbm, x_ref, s_in.at[0])
@@ -211,7 +222,7 @@
         [jnp.concatenate([rh, rh], axis=1), jnp.concatenate([rl, rl], axis=1)], axis=0
     )
     for q in range(nxk):
-        eh, el = split2(err_ref[:, q].reshape(ch, 128))
+        eh, el = split2(slots(err_ref[:, q]))
         rows = jnp.concatenate([eh, el], axis=1)
         if ch < 256:
             rows = jnp.concatenate([rows, jnp.zeros((256 - ch, 256), BF16)], axis=0)
@@ -228,6 +239,15 @@
     ghs[POS:, :] = jnp.zeros((LP - POS, 128), BF16)
 
     load_gh.wait()
+    halves_of = jnp.concatenate([ghp[0 : POS // 2, :], ghp[POS // 2 : POS, :]], axis=1)
+    ght[...] = jnp.concatenate(
+        [
+            jnp.zeros((64, 256), BF16),
+            halves_of,
+            jnp.zeros((LX - 512 - 64 - POS // 2, 256), BF16),
+        ],
+        axis=0,
+    )
     in_gh.wait_recv()
     in_r.wait_recv()
     sh, sl = split2(rs[...])
@@ -286,11 +306,7 @@
     gt_copy.start()
 
     loop(1, nz, lambda s: cz_copy(s).wait_recv())
-    for zz in range(nz):
-        first, last = unpack(cz[zz])
-        conv32[OWN * zz : OWN * zz + 16, :] = first
-        conv32[OWN * zz + 16 : OWN * zz + 24, :] = last
-    cvf[x, k] = conv32[...].astype(BF16)
+    cvf[x, k] = cz[...]
 
     gt_copy.wait_recv()
     groups = []
@@ -298,12 +314,29 @@
         groups.append(
             jnp.concatenate([gt[rg // 2, (rg % 2) * 5 + j] for j in range(5)], axis=1)
         )
-    gsplit = jnp.concatenate(split2(jnp.concatenate(groups, axis=0)), axis=0)
-    conv_pad = cvf[x, k]
-    if ch < 256:
-        conv_pad = jnp.concatenate([conv_pad, jnp.zeros((256 - ch, LP), BF16)], axis=0)
-    conv_left = dot(gsplit, conv_pad, NT)
-    conv_left = conv_left[0:32] + conv_left[32:64]
+    gfull = jnp.concatenate(groups, axis=0)
+    lane_g = lax.broadcasted_iota(jnp.int32, (32, LP), 1)
+    inside = (lane_g >= 64) & (lane_g < 64 + POS // 2)
+    glow = jnp.where(inside, pltpu.roll(gfull, 64, 1), 0.0)[:, 0 : LX - 512]
+    ghigh = jnp.where(inside, pltpu.roll(gfull, LP + 64 - POS // 2, 1), 0.0)[:, 0 : LX - 512]
+    packed = cz[...]
+    halves = packed[:, :, 512:].astype(F32)
+    conv_top = dot(
+        jnp.concatenate(split2(gfull), axis=0), packed[:, :, 0:LP].reshape(top, LP), NT
+    )
+    conv_last = None
+    for part, rows in ((glow, halves[:, 0:8]), (ghigh, halves[:, 8:16])):
+        rows = rows.reshape(ch - top, LX - 512).astype(BF16)
+        term = dot(jnp.concatenate(split2(part), axis=0), rows, NT)
+        conv_last = term if conv_last is None else conv_last + term
+    conv_left = jnp.concatenate(
+        [
+            conv_top[0:32] + conv_top[32:64],
+            conv_last[0:32] + conv_last[32:64],
+            jnp.zeros((32, 256 - ch), F32),
+        ],
+        axis=1,
+    )
     for rg in range(4):
         for part in range(2):
             st[2 * rg + part] += conv_left[8 * rg : 8 * rg + 8, 128 * part : 128 * part + 128]
@@ -356,8 +389,12 @@
 
     def local_grad(xx, kk):
         q = xx * 2 + kk
-        part = dot(cvf[xx, kk], ghp[...], NN) + err_ref[:, q].reshape(ch, 128)
-        cor[:, q] = part.reshape(nz, OWN, 128)
+        packed = cvf[xx, kk].reshape(top, LX)
+        first = dot(packed[:, 0:LP], ghp[...], NN)
+        both = dot(packed[:, 512:], ght[...], NN).reshape(nz, 16, 256)
+        last = both[:, 0:8, 0:128] + both[:, 8:16, 128:256]
+        part = jnp.concatenate([first, last.reshape(ch - top, 128)], axis=0) + slots(err_ref[:, q])
+        cor[:, q] = natural_rows(part)
         chl[q, 0:ch, :] = jnp.concatenate(split2(part), axis=1)
 
     if ch < 256:
@@ -427,12 +464,12 @@
     loop(1, nz, lambda s: lz_copy(s).start())
 
     cx_copies[0].wait_recv()
-    part0 = cvf.at[left_x, k, pl.ds(0, half)]
+    part0 = cvf.at[left_x, k, pl.ds(0, nz // 2)]
     cx_copies.append(copy(part0, part0, s_cx.at[2], r_cx.at[2], at_x(right_x)))
     cx_copies[2].start()
     cc_copy(1).start()
     cx_copies[1].wait_recv()
-    part1 = cvf.at[right_x, k, pl.ds(half, half)]
+    part1 = cvf.at[right_x, k, pl.ds(nz // 2, nz // 2)]
     cx_copies.append(copy(part1, part1, s_cx.at[3], r_cx.at[3], at_x(left_x)))
     cx_copies[3].start()
     cc_copy(2).start()
@@ -485,7 +522,7 @@
         term = term[0:32] + term[32:64] + term[64:96]
         gram = term if gram is None else gram + term
     for q in range(nxk):
-        lsn[:, q] = lefts[q].T[0:ch].reshape(nz, OWN, RANK)
+        lsn[:, q] = natural_rows(lefts[q].T)
     natural = lsn[...].reshape(channels, RANK).T
     nh, nm, nl = split3(natural)
     ls4[...] = jnp.concatenate([nh, nm, nh, nm], axis=0).T
@@ -590,12 +627,47 @@
         one.wait_send()
 
 
-def finish(kg_ref, left_ref, right_ref, w_ref, ls_ref, cor_ref, kg_out, left_out, right_out, err_out):
-    kg_out[...] = kg_ref[...]
-    left_out[...] = left_ref[...]
-    right_out[...] = right_ref[...]
-    approx = dot(ls_ref[...], w_ref[...], NN)
-    err_out[...] = cor_ref[...] - approx.reshape(cor_ref.shape)
+def finish(
+    kg_hbm, left_hbm, right_hbm, w_hbm, ls_hbm, cor_hbm, kg_out, left_out, right_out, err_out,
+    w_ref, ls_ref, cor_ref, load_sems, store_sems, small_sems,
+):
+    count = load_sems.shape[0] - 1
+    width = cor_ref.shape[0] // count
+    rows = ls_ref.shape[0] // count
+    small = [
+        pltpu.make_async_copy(a, b, small_sems.at[i])
+        for i, (a, b) in enumerate(((kg_hbm, kg_out), (left_hbm, left_out), (right_hbm, right_out)))
+    ]
+    w_load = pltpu.make_async_copy(w_hbm, w_ref, load_sems.at[count, 0])
+    w_load.start()
+    loads = []
+    for i in range(count):
+        at, lines = pl.ds(i * width, width), pl.ds(i * rows, rows)
+        loads.append(
+            (
+                pltpu.make_async_copy(ls_hbm.at[lines], ls_ref.at[lines], load_sems.at[i, 0]),
+                pltpu.make_async_copy(cor_hbm.at[at], cor_ref.at[at], load_sems.at[i, 1]),
+            )
+        )
+        for one in loads[i]:
+            one.start()
+    for one in small:
+        one.start()
+    w_load.wait()
+    stores = []
+    for i in range(count):
+        for one in loads[i]:
+            one.wait()
+        at, lines = slice(i * width, (i + 1) * width), slice(i * rows, (i + 1) * rows)
+        approx = dot(ls_ref[lines, :], w_ref[...], NN)
+        cor_ref[at] = cor_ref[at] - approx.reshape((width,) + cor_ref.shape[1:])
+        part = pl.ds(i * width, width)
+        stores.append(
+            pltpu.make_async_copy(cor_ref.at[part], err_out.at[part], store_sems.at[i])
+        )
+        stores[i].start()
+    for one in stores + small:
+        one.wait()
 
 
 def on_device(ny, nz, nx, block_input, depth_kernel, w_expand, grad_hidden, error_old, right_init):
@@ -613,6 +685,7 @@
         vmem((RANK, 128), F32),
         vmem((LP, 128), BF16),
         vmem((LP, 128), BF16),
+        vmem((LX - 512, 256), BF16),
         vmem((channels, 128), BF16),
         vmem((RANK, 128), F32),
         vmem((nz, nx, 2, OWN, 256), F32),
@@ -625,8 +698,7 @@
         vmem((8, LP), F32),
         vmem((64, channels), F32),
         vmem((OWN, 64), F32),
-        vmem((ch, LP), F32),
-        vmem((nx, 2, ch, LP), BF16),
+        vmem((nx, 2, nz, 16, LX), BF16),
         vmem((2, ch, LP), F32),
         vmem((3, ch, LP), BF16),
         vmem((2, ch // 2, LP), BF16),
@@ -685,11 +757,20 @@
         error_old.reshape(nz, nxk, OWN, 128),
         right_init.T,
     )
+    steps = min(4, nz)
     kg, left, right, err = pl.pallas_call(
         finish,
         out_shape=mids[0:3] + (cor_shape,),
-        in_specs=[spec] * 6,
-        out_specs=(spec,) * 4,
+        in_specs=[far] * 6,
+        out_specs=(far,) * 4,
+        scratch_shapes=[
+            vmem((4 * RANK, 128), BF16),
+            vmem((channels, 4 * RANK), BF16),
+            vmem((nz, nxk, OWN, 128), F32),
+            pltpu.SemaphoreType.DMA((steps + 1, 2)),
+            pltpu.SemaphoreType.DMA((steps,)),
+            pltpu.SemaphoreType.DMA((3,)),
+        ],
         compiler_params=pltpu.CompilerParams(vmem_limit_bytes=60 * 1024 * 1024),
         cost_estimate=pl.CostEstimate(
             flops=60_000_000, bytes_accessed=2_500_000, transcendentals=0

time: 59.4 us -> 64.6 us (1.088)
  Pallas kernels: 58.6 us -> 63.8 us
    pallas_call x1, Pallas kernels: 2.57 us -> 8.48 us  [on_device(): pl.pallas_call(finish, out_shape=mids[0:3] + (cor_shape,), in_specs=[far]...]
    pallas_call x1, Pallas kernels: 56 us -> 55.3 us  [on_device(): pl.pallas_call(functools.partial(kernel, ny, nz, nx), out_shape=mids, in_...]
where the time goes in v6:
time: 64.6 us; the launch traced here: 64.5 us
  Pallas kernels  63.8 us (99%)
    pallas_call x1, Pallas kernels, on_device(): pl.pallas_call(functools.partial(kernel, ny, nz, nx), out_shape=mids, in_...  55.3 us
    pallas_call x1, Pallas kernels, on_device(): pl.pallas_call(finish, out_shape=mids[0:3] + (cor_shape,), in_specs=[far]...  8.48 us

profile of v6, /device:TPU:1, one launch (start us, length us, event | category | flops | bytes accessed | tf_op | source)
XLA Modules:
  0.0 64.5 jit_solution(5963295308165505412)
XLA Ops:
  0.6 55.3 %shard_map.93 = (f32[7,7,24]{2,1,0:T(8,128)}, f32[32,1536]{1,0:T(8,128)}, f32[32,128]{1,0:T(8,128)}, bf16[128,128]{1,0:T(8,128)(2,1)}, bf16[1536,128]{1,0:T(8,128)(2,1)}, /*index=5*/f32[8,8,24,128]{3,2,1,0:T(8,128)}) custom-call(bf16[24,24,24]{2,1,0:T(8,128)(2,1)} %bitcast.10, f32[7,7,1536]{2,1,0:T(8,128)} %k_hbm.1, bf16[1536,128]{1,0:T(8,128)(2,1)} %w_hbm.1, ...), custom_call_target="tpu_custom_call" | custom-call | flops 600000000 | bytes 4000000 | tf_op jit(solution)/shard_map/pallas_call | solution.py:740
  56.0 8.5 %shard_map.94 = (f32[7,7,24]{2,1,0:T(8,128)}, f32[32,1536]{1,0:T(8,128)}, f32[32,128]{1,0:T(8,128)}, f32[8,8,24,128]{3,2,1,0:T(8,128)}) custom-call(f32[7,7,24]{2,1,0:T(8,128)} %get-tuple-element.14.kg_hbm, f32[32,1536]{1,0:T(8,128)} %get-tuple-element.15.left_hbm, f32[32,128]{1,0:T(8,128)} %get-tuple-element.16.right_hbm, ...), custom_call_target="tpu_custom_call" | custom-call | flops 60000000 | bytes 2500000 | tf_op jit(solution)/shard_map/pallas_call | solution.py:761

commit v7 on v6

--- a/solution.py
+++ b/solution.py
@@ -413,6 +413,31 @@
 
     local_grad(x, k)
 
+    def lx_wait(s):
+        got = ll.at[k, z, lax.rem(x - s + nx, nx)]
+        copy(got, got, s_lx.at[s], r_lx.at[s], at_x(lax.rem(x + s, nx))).wait_recv()
+
+    loop(1, nx, lx_wait)
+
+    def lz_copy(s):
+        own = ll.at[k, z]
+        return copy(own, own, s_lz.at[s], r_lz.at[s], at_z(zpeer(s)))
+
+    loop(1, nz, lambda s: lz_copy(s).start())
+
+    cx_copies[0].wait_recv()
+    part0 = cvf.at[left_x, k, pl.ds(0, nz // 2)]
+    cx_copies.append(copy(part0, part0, s_cx.at[2], r_cx.at[2], at_x(right_x)))
+    cx_copies[2].start()
+    cc_copy(1).start()
+    cx_copies[1].wait_recv()
+    part1 = cvf.at[right_x, k, pl.ds(nz // 2, nz // 2)]
+    cx_copies.append(copy(part1, part1, s_cx.at[3], r_cx.at[3], at_x(left_x)))
+    cx_copies[3].start()
+    cc_copy(2).start()
+    local_grad(left_x, k)
+    local_grad(right_x, k)
+
     loop(1, nz, lambda s: xz_copy(s).wait_recv())
     xp[:, 0:128] = jnp.zeros((ch, 128), F32)
     xp[:, 128 + LP :] = jnp.zeros((ch, LX - 128 - LP), F32)
@@ -451,45 +476,9 @@
     loop(1, nz, lambda s: rk_copy(s).start())
     rk[z] = kgt[z]
 
-    def lx_wait(s):
-        got = ll.at[k, z, lax.rem(x - s + nx, nx)]
-        copy(got, got, s_lx.at[s], r_lx.at[s], at_x(lax.rem(x + s, nx))).wait_recv()
-
-    loop(1, nx, lx_wait)
-
-    def lz_copy(s):
-        own = ll.at[k, z]
-        return copy(own, own, s_lz.at[s], r_lz.at[s], at_z(zpeer(s)))
-
-    loop(1, nz, lambda s: lz_copy(s).start())
-
-    cx_copies[0].wait_recv()
-    part0 = cvf.at[left_x, k, pl.ds(0, nz // 2)]
-    cx_copies.append(copy(part0, part0, s_cx.at[2], r_cx.at[2], at_x(right_x)))
-    cx_copies[2].start()
-    cc_copy(1).start()
-    cx_copies[1].wait_recv()
-    part1 = cvf.at[right_x, k, pl.ds(nz // 2, nz // 2)]
-    cx_copies.append(copy(part1, part1, s_cx.at[3], r_cx.at[3], at_x(left_x)))
-    cx_copies[3].start()
-    cc_copy(2).start()
-    local_grad(left_x, k)
-    local_grad(right_x, k)
-
     for s in range(3):
         cc_copy(s).wait_recv()
         local_grad(sources[s], 1 - k)
-
-    loop(1, nz, lambda s: rk_copy(s).wait_recv())
-    total = rk[0]
-    for q in range(1, nz):
-        total = total + rk[q]
-    yk[y] = total
-
-    def yk_copy(s):
-        return copy(yk.at[y], yk.at[y], s_yk.at[s], r_yk.at[s], at_y(lax.rem(y + s, ny)))
-
-    loop(1, ny, lambda s: yk_copy(s).start())
 
     def lz_wait(s):
         got = ll.at[k, lax.rem(z - s + nz, nz)]
@@ -545,6 +534,17 @@
         return copy(rp.at[y], rp.at[y], s_rp.at[s], r_rp.at[s], at_y(lax.rem(y + s, ny)))
 
     loop(1, ny, lambda s: rp_copy(s).start())
+
+    loop(1, nz, lambda s: rk_copy(s).wait_recv())
+    total = rk[0]
+    for q in range(1, nz):
+        total = total + rk[q]
+    yk[y] = total
+
+    def yk_copy(s):
+        return copy(yk.at[y], yk.at[y], s_yk.at[s], r_yk.at[s], at_y(lax.rem(y + s, ny)))
+
+    loop(1, ny, lambda s: yk_copy(s).start())
 
     row_id = lax.broadcasted_iota(jnp.int32, (RANK, RANK), 0)
     lane_id = lax.broadcasted_iota(jnp.int32, (RANK, RANK), 1)
@@ -629,14 +629,21 @@
 
 def finish(
     kg_hbm, left_hbm, right_hbm, w_hbm, ls_hbm, cor_hbm, kg_out, left_out, right_out, err_out,
-    w_ref, ls_ref, cor_ref, load_sems, store_sems, small_sems,
+    w_ref, ls_ref, cor_ref, kg_ref, left_ref, right_ref, load_sems, store_sems, small_sems,
 ):
     count = load_sems.shape[0] - 1
     width = cor_ref.shape[0] // count
     rows = ls_ref.shape[0] // count
-    small = [
-        pltpu.make_async_copy(a, b, small_sems.at[i])
-        for i, (a, b) in enumerate(((kg_hbm, kg_out), (left_hbm, left_out), (right_hbm, right_out)))
+    small = (
+        (kg_hbm, kg_ref, kg_out),
+        (left_hbm, left_ref, left_out),
+        (right_hbm, right_ref, right_out),
+    )
+    small_loads = [
+        pltpu.make_async_copy(a, b, small_sems.at[i, 0]) for i, (a, b, _) in enumerate(small)
+    ]
+    small_stores = [
+        pltpu.make_async_copy(b, c, small_sems.at[i, 1]) for i, (_, b, c) in enumerate(small)
     ]
     w_load = pltpu.make_async_copy(w_hbm, w_ref, load_sems.at[count, 0])
     w_load.start()
@@ -651,7 +658,7 @@
         )
         for one in loads[i]:
             one.start()
-    for one in small:
+    for one in small_loads:
         one.start()
     w_load.wait()
     stores = []
@@ -666,7 +673,11 @@
             pltpu.make_async_copy(cor_ref.at[part], err_out.at[part], store_sems.at[i])
         )
         stores[i].start()
-    for one in stores + small:
+        if i == 0:
+            for load, store in zip(small_loads, small_stores):
+                load.wait()
+                store.start()
+    for one in stores + small_stores:
         one.wait()
 
 
@@ -767,9 +778,12 @@
             vmem((4 * RANK, 128), BF16),
             vmem((channels, 4 * RANK), BF16),
             vmem((nz, nxk, OWN, 128), F32),
+            vmem((7, 7, OWN), F32),
+            vmem((RANK, channels), F32),
+            vmem((RANK, 128), F32),
             pltpu.SemaphoreType.DMA((steps + 1, 2)),
             pltpu.SemaphoreType.DMA((steps,)),
-            pltpu.SemaphoreType.DMA((3,)),
+            pltpu.SemaphoreType.DMA((3, 2)),
         ],
         compiler_params=pltpu.CompilerParams(vmem_limit_bytes=60 * 1024 * 1024),
         cost_estimate=pl.CostEstimate(

time: 64.6 us -> 59.8 us (0.926)
  Pallas kernels: 63.8 us -> 59 us
    pallas_call x1, Pallas kernels: 8.48 us -> 2.78 us  [on_device(): pl.pallas_call(finish, out_shape=mids[0:3] + (cor_shape,), in_specs=[far]...]
    pallas_call x1, Pallas kernels: 55.3 us -> 56.2 us  [on_device(): pl.pallas_call(functools.partial(kernel, ny, nz, nx), out_shape=mids, in_...]
where the time goes in v7:
time: 59.8 us; the launch traced here: 59.6 us
  Pallas kernels  59 us (99%)
  between operations  0.64 us (1%)
    pallas_call x1, Pallas kernels, on_device(): pl.pallas_call(functools.partial(kernel, ny, nz, nx), out_shape=mids, in_...  56.2 us
    pallas_call x1, Pallas kernels, on_device(): pl.pallas_call(finish, out_shape=mids[0:3] + (cor_shape,), in_specs=[far]...  2.78 us

profile of v7, /device:TPU:1, one launch (start us, length us, event | category | flops | bytes accessed | tf_op | source)
XLA Modules:
  0.0 59.6 jit_solution(4027527485898364627)
XLA Ops:
  0.6 56.2 %shard_map.93 = (f32[7,7,24]{2,1,0:T(8,128)}, f32[32,1536]{1,0:T(8,128)}, f32[32,128]{1,0:T(8,128)}, bf16[128,128]{1,0:T(8,128)(2,1)}, bf16[1536,128]{1,0:T(8,128)(2,1)}, /*index=5*/f32[8,8,24,128]{3,2,1,0:T(8,128)}) custom-call(bf16[24,24,24]{2,1,0:T(8,128)(2,1)} %bitcast.10, f32[7,7,1536]{2,1,0:T(8,128)} %k_hbm.1, bf16[1536,128]{1,0:T(8,128)(2,1)} %w_hbm.1, ...), custom_call_target="tpu_custom_call" | custom-call | flops 600000000 | bytes 4000000 | tf_op jit(solution)/shard_map/pallas_call | solution.py:751
  56.8 2.8 %shard_map.94 = (f32[7,7,24]{2,1,0:T(8,128)}, f32[32,1536]{1,0:T(8,128)}, f32[32,128]{1,0:T(8,128)}, f32[8,8,24,128]{3,2,1,0:T(8,128)}) custom-call(f32[7,7,24]{2,1,0:T(8,128)} %get-tuple-element.14.kg_hbm, f32[32,1536]{1,0:T(8,128)} %get-tuple-element.15.left_hbm, f32[32,128]{1,0:T(8,128)} %get-tuple-element.16.right_hbm, ...), custom_call_target="tpu_custom_call" | custom-call | flops 60000000 | bytes 2500000 | tf_op jit(solution)/shard_map/pallas_call | solution.py:772

commit v8 on v6

--- a/solution.py
+++ b/solution.py
@@ -56,9 +56,9 @@
     kg_out, left_out, right_out, w_out, ls4_out, cor_out,
     x_ref, k_ref, w_ref, err_ref, r_ref,
     ghp, ghs, ght, ws, rs, wf, x2, xo, conv24, cz, xz, xp, mk, kflat, kt, cvf, gr, gb, rh1, rh2, g32,
-    eg, gg, es, cs, gt, st, rz, ys, ll, chl, rp, kgt, rk, yk, lsn, ls4, cor, left,
+    eg, gg, es, cs, cg, gt, st, rz, ys, ll, chl, rp, kgt, rk, yk, lsn, ls4, cor, left,
     s_in,
-    s_cz, r_cz, s_xz, r_xz, s_es, r_es, s_cs, r_cs, s_gt, r_gt, s_rz, r_rz, s_ys, r_ys, s_lx, r_lx, s_lz, r_lz,
+    s_cz, r_cz, s_xz, r_xz, s_es, r_es, s_cs, r_cs, s_cg, r_cg, s_gt, r_gt, s_rz, r_rz, s_ys, r_ys, s_lx, r_lx, s_lz, r_lz,
     s_lk, r_lk, s_rp, r_rp, s_rk, r_rk, s_yk, r_yk, s_in2, r_in2, s_gx, r_gx, s_cx, r_cx, s_cc, r_cc,
 ):
     nxk = 2 * nx
@@ -259,11 +259,17 @@
         for j in range(5):
             gg[rg // 2, (rg % 2) * 5 + j] = g[8 * rg : 8 * rg + 8, 128 * j : 128 * j + 128]
 
+    cg[x] = gg[k]
+
+    def cg_copy(s):
+        return copy(cg.at[x], cg.at[x], s_cg.at[s], r_cg.at[s], at_x(lax.rem(x + s, nx)))
+
+    loop(1, nx, lambda s: cg_copy(s).start())
+
     es_copy.wait_recv()
 
     def chip_sum(xx):
-        cs[xx, 0, 0:8] = eg[xx, k] + es[xx]
-        cs[xx, 0, 8:18] = gg[k]
+        cs[xx, 0] = eg[xx, k] + es[xx]
 
     loop(0, nx, chip_sum)
     cs[x, 1] = cs[x, 0]
@@ -296,14 +302,23 @@
     gr[1] = grad_rows(left_x)
     g32[...] = grad_rows(x)
 
+    def cg_wait(s):
+        got = cg.at[lax.rem(x - s + nx, nx)]
+        copy(got, got, s_cg.at[s], r_cg.at[s], at_x(lax.rem(x + s, nx))).wait_recv()
+
+    loop(1, nx, cg_wait)
+    total = cg[0]
+    for q in range(1, nx):
+        total = total + cg[q]
+    gt[k] = total
+    gt_copy = copy(gt.at[k], gt.at[k], s_gt.at[0], r_gt.at[0], sibling)
+    gt_copy.start()
+
     loop(1, nx, lambda s: cs_copy(s).wait_recv())
     total = cs[0, 1]
     for q in range(1, nx):
         total = total + cs[q, 1]
-    st[...] = total[0:8]
-    gt[k] = total[8:18]
-    gt_copy = copy(gt.at[k], gt.at[k], s_gt.at[0], r_gt.at[0], sibling)
-    gt_copy.start()
+    st[...] = total
 
     loop(1, nz, lambda s: cz_copy(s).wait_recv())
     cvf[x, k] = cz[...]
@@ -611,6 +626,7 @@
     for one in (in_r, in_gh, in_w):
         one.wait_send()
     loop(1, nx, lambda s: cs_copy(s).wait_send())
+    loop(1, nx, lambda s: cg_copy(s).wait_send())
     gt_copy.wait_send()
     loop(1, nz, lambda s: rz_copy(s).wait_send())
     loop(1, ny, lambda s: ys_copy(s).wait_send())
@@ -627,47 +643,12 @@
         one.wait_send()
 
 
-def finish(
-    kg_hbm, left_hbm, right_hbm, w_hbm, ls_hbm, cor_hbm, kg_out, left_out, right_out, err_out,
-    w_ref, ls_ref, cor_ref, load_sems, store_sems, small_sems,
-):
-    count = load_sems.shape[0] - 1
-    width = cor_ref.shape[0] // count
-    rows = ls_ref.shape[0] // count
-    small = [
-        pltpu.make_async_copy(a, b, small_sems.at[i])
-        for i, (a, b) in enumerate(((kg_hbm, kg_out), (left_hbm, left_out), (right_hbm, right_out)))
-    ]
-    w_load = pltpu.make_async_copy(w_hbm, w_ref, load_sems.at[count, 0])
-    w_load.start()
-    loads = []
-    for i in range(count):
-        at, lines = pl.ds(i * width, width), pl.ds(i * rows, rows)
-        loads.append(
-            (
-                pltpu.make_async_copy(ls_hbm.at[lines], ls_ref.at[lines], load_sems.at[i, 0]),
-                pltpu.make_async_copy(cor_hbm.at[at], cor_ref.at[at], load_sems.at[i, 1]),
-            )
-        )
-        for one in loads[i]:
-            one.start()
-    for one in small:
-        one.start()
-    w_load.wait()
-    stores = []
-    for i in range(count):
-        for one in loads[i]:
-            one.wait()
-        at, lines = slice(i * width, (i + 1) * width), slice(i * rows, (i + 1) * rows)
-        approx = dot(ls_ref[lines, :], w_ref[...], NN)
-        cor_ref[at] = cor_ref[at] - approx.reshape((width,) + cor_ref.shape[1:])
-        part = pl.ds(i * width, width)
-        stores.append(
-            pltpu.make_async_copy(cor_ref.at[part], err_out.at[part], store_sems.at[i])
-        )
-        stores[i].start()
-    for one in stores + small:
-        one.wait()
+def finish(kg_ref, left_ref, right_ref, w_ref, ls_ref, cor_ref, kg_out, left_out, right_out, err_out):
+    kg_out[...] = kg_ref[...]
+    left_out[...] = left_ref[...]
+    right_out[...] = right_ref[...]
+    approx = dot(ls_ref[...], w_ref[...], NN)
+    err_out[...] = cor_ref[...] - approx.reshape(cor_ref.shape)
 
 
 def on_device(ny, nz, nx, block_input, depth_kernel, w_expand, grad_hidden, error_old, right_init):
@@ -707,7 +688,8 @@
         vmem((nx, 2, 8, 8, 128), F32),
         vmem((2, 10, 8, 128), F32),
         vmem((nx, 8, 8, 128), F32),
-        vmem((nx, 2, 18, 8, 128), F32),
+        vmem((nx, 2, 8, 8, 128), F32),
+        vmem((nx, 10, 8, 128), F32),
         vmem((2, 10, 8, 128), F32),
         vmem((8, 8, 128), F32),
         vmem((nz, tpz, 8, 128), F32),
@@ -724,7 +706,7 @@
         vmem((RANK, channels), F32),
     ]
     sems = [pltpu.SemaphoreType.DMA((9,))]
-    for count in (nz, nz, 2, nx, 1, nz, ny, nx, nz, 1, ny, nz, ny, 4, 4, 4, 4):
+    for count in (nz, nz, 2, nx, nx, 1, nz, ny, nx, nz, 1, ny, nz, ny, 4, 4, 4, 4):
         sems += [pltpu.SemaphoreType.DMA((count,))] * 2
     spec = pl.BlockSpec(memory_space=pltpu.VMEM)
     far = pl.BlockSpec(memory_space=pl.ANY)
@@ -757,20 +739,11 @@
         error_old.reshape(nz, nxk, OWN, 128),
         right_init.T,
     )
-    steps = min(4, nz)
     kg, left, right, err = pl.pallas_call(
         finish,
         out_shape=mids[0:3] + (cor_shape,),
-        in_specs=[far] * 6,
-        out_specs=(far,) * 4,
-        scratch_shapes=[
-            vmem((4 * RANK, 128), BF16),
-            vmem((channels, 4 * RANK), BF16),
-            vmem((nz, nxk, OWN, 128), F32),
-            pltpu.SemaphoreType.DMA((steps + 1, 2)),
-            pltpu.SemaphoreType.DMA((steps,)),
-            pltpu.SemaphoreType.DMA((3,)),
-        ],
+        in_specs=[spec] * 6,
+        out_specs=(spec,) * 4,
         compiler_params=pltpu.CompilerParams(vmem_limit_bytes=60 * 1024 * 1024),
         cost_estimate=pl.CostEstimate(
             flops=60_000_000, bytes_accessed=2_500_000, transcendentals=0

time: 64.6 us -> 58.4 us (0.904)
  Pallas kernels: 63.8 us -> 57.6 us
    pallas_call x1, Pallas kernels: 8.48 us -> 2.58 us  [on_device(): pl.pallas_call(finish, out_shape=mids[0:3] + (cor_shape,), in_specs=[spec...]
where the time goes in v8:
time: 58.4 us; the launch traced here: 58.3 us
  Pallas kernels  57.6 us (99%)
  between operations  0.64 us (1%)
    pallas_call x1, Pallas kernels, on_device(): pl.pallas_call(functools.partial(kernel, ny, nz, nx), out_shape=mids, in_...  55.1 us
    pallas_call x1, Pallas kernels, on_device(): pl.pallas_call(finish, out_shape=mids[0:3] + (cor_shape,), in_specs=[spec...  2.58 us

profile of v8, /device:TPU:1, one launch (start us, length us, event | category | flops | bytes accessed | tf_op | source)
XLA Modules:
  0.0 58.3 jit_solution(982583559351270160)
XLA Ops:
  0.6 55.1 %shard_map.93 = (f32[7,7,24]{2,1,0:T(8,128)}, f32[32,1536]{1,0:T(8,128)}, f32[32,128]{1,0:T(8,128)}, bf16[128,128]{1,0:T(8,128)(2,1)}, bf16[1536,128]{1,0:T(8,128)(2,1)}, /*index=5*/f32[8,8,24,128]{3,2,1,0:T(8,128)}) custom-call(bf16[24,24,24]{2,1,0:T(8,128)(2,1)} %bitcast.10, f32[7,7,1536]{2,1,0:T(8,128)} %k_hbm.1, bf16[1536,128]{1,0:T(8,128)(2,1)} %w_hbm.1, ...), custom_call_target="tpu_custom_call" | custom-call | flops 600000000 | bytes 4000000 | tf_op jit(solution)/shard_map/pallas_call | solution.py:722
  55.7 2.6 %shard_map.94 = (f32[7,7,24]{2,1,0:T(8,128)}, f32[32,1536]{1,0:T(8,128)}, f32[32,128]{1,0:T(8,128)}, f32[8,8,24,128]{3,2,1,0:T(8,128)}) custom-call(f32[7,7,24]{2,1,0:T(8,128)} %get-tuple-element.14.kg_ref, f32[32,1536]{1,0:T(8,128)} %get-tuple-element.15.left_ref, f32[32,128]{1,0:T(8,128)} %get-tuple-element.16.right_ref, ...), custom_call_target="tpu_custom_call" | custom-call | flops 60000000 | bytes 2500000 | tf_op jit(solution)/shard_map/pallas_call | solution.py:742

commit v9 on v8

--- a/solution.py
+++ b/solution.py
@@ -36,6 +36,11 @@
         return carry
 
     lax.fori_loop(lo, hi, step, 0, unroll=unroll)
+
+
+def each_peer(count, body):
+    for s in sorted(range(1, count), key=lambda s: -min(s, count - s)):
+        body(s)
 
 
 def split2(v):
@@ -202,7 +207,7 @@
 
     pl.semaphore_wait(barrier, (nz - 1) + (nx - 1) + (ny - 1) + 1)
 
-    loop(1, nz, lambda s: cz_copy(s).start())
+    each_peer(nz, lambda s: cz_copy(s).start())
 
     in_gh = copy(gh_hbm, ghs.at[pl.ds(0, POS)], s_in2.at[0], r_in2.at[0], sibling)
     in_r = copy(r_hbm, rs, s_in2.at[1], r_in2.at[1], sibling)
@@ -264,7 +269,7 @@
     def cg_copy(s):
         return copy(cg.at[x], cg.at[x], s_cg.at[s], r_cg.at[s], at_x(lax.rem(x + s, nx)))
 
-    loop(1, nx, lambda s: cg_copy(s).start())
+    each_peer(nx, lambda s: cg_copy(s).start())
 
     es_copy.wait_recv()
 
@@ -278,7 +283,7 @@
         xx = lax.rem(x + s, nx)
         return copy(cs.at[xx, 0], cs.at[x, 1], s_cs.at[s], r_cs.at[s], at_x(xx))
 
-    loop(1, nx, lambda s: cs_copy(s).start())
+    each_peer(nx, lambda s: cs_copy(s).start())
 
     load_w.wait()
     in_w.wait_recv()
@@ -360,7 +365,7 @@
         zz = zpeer(s)
         return copy(st.at[pl.ds(zz * tpz, tpz)], rz.at[z], s_rz.at[s], r_rz.at[s], at_z(zz))
 
-    loop(1, nz, lambda s: rz_copy(s).start())
+    each_peer(nz, lambda s: rz_copy(s).start())
     rz[z] = st[pl.ds(z * tpz, tpz)]
     loop(1, nz, lambda s: xz_copy(s).start())
 
@@ -391,7 +396,7 @@
 
     cc_copy(0).start()
 
-    loop(1, nz, lambda s: rz_copy(s).wait_recv())
+    each_peer(nz, lambda s: rz_copy(s).wait_recv())
     total = rz[0]
     for q in range(1, nz):
         total = total + rz[q]
@@ -400,7 +405,7 @@
     def ys_copy(s):
         return copy(ys.at[y], ys.at[y], s_ys.at[s], r_ys.at[s], at_y(lax.rem(y + s, ny)))
 
-    loop(1, ny, lambda s: ys_copy(s).start())
+    each_peer(ny, lambda s: ys_copy(s).start())
 
     def local_grad(xx, kk):
         q = xx * 2 + kk
@@ -414,7 +419,7 @@
 
     if ch < 256:
         chl[:, ch:, :] = jnp.zeros((nxk, 256 - ch, 256), BF16)
-    loop(1, ny, lambda s: ys_copy(s).wait_recv())
+    each_peer(ny, lambda s: ys_copy(s).wait_recv())
     total = ys[0]
     for q in range(1, ny):
         total = total + ys[q]
@@ -424,7 +429,7 @@
         own = ll.at[k, z, x]
         return copy(own, own, s_lx.at[s], r_lx.at[s], at_x(lax.rem(x + s, nx)))
 
-    loop(1, nx, lambda s: lx_copy(s).start())
+    each_peer(nx, lambda s: lx_copy(s).start())
 
     local_grad(x, k)
 
@@ -463,7 +468,7 @@
         zz = zpeer(s)
         return copy(kgt.at[zz], rk.at[z], s_rk.at[s], r_rk.at[s], at_z(zz))
 
-    loop(1, nz, lambda s: rk_copy(s).start())
+    each_peer(nz, lambda s: rk_copy(s).start())
     rk[z] = kgt[z]
 
     def lx_wait(s):
@@ -476,7 +481,7 @@
         own = ll.at[k, z]
         return copy(own, own, s_lz.at[s], r_lz.at[s], at_z(zpeer(s)))
 
-    loop(1, nz, lambda s: lz_copy(s).start())
+    each_peer(nz, lambda s: lz_copy(s).start())
 
     cx_copies[0].wait_recv()
     part0 = cvf.at[left_x, k, pl.ds(0, nz // 2)]
@@ -504,7 +509,7 @@
     def yk_copy(s):
         return copy(yk.at[y], yk.at[y], s_yk.at[s], r_yk.at[s], at_y(lax.rem(y + s, ny)))
 
-    loop(1, ny, lambda s: yk_copy(s).start())
+    each_peer(ny, lambda s: yk_copy(s).start())
 
     def lz_wait(s):
         got = ll.at[k, lax.rem(z - s + nz, nz)]
@@ -559,7 +564,7 @@
     def rp_copy(s):
         return copy(rp.at[y], rp.at[y], s_rp.at[s], r_rp.at[s], at_y(lax.rem(y + s, ny)))
 
-    loop(1, ny, lambda s: rp_copy(s).start())
+    each_peer(ny, lambda s: rp_copy(s).start())
 
     row_id = lax.broadcasted_iota(jnp.int32, (RANK, RANK), 0)
     lane_id = lax.broadcasted_iota(jnp.int32, (RANK, RANK), 1)
@@ -601,7 +606,7 @@
     ah, am, al = split3(jnp.concatenate([linv, inverse], axis=0))
     final_left = jnp.concatenate([ah, ah, ah, am, am, al], axis=1)
 
-    loop(1, ny, lambda s: rp_copy(s).wait_recv())
+    each_peer(ny, lambda s: rp_copy(s).wait_recv())
     total = rp[0]
     for q in range(1, ny):
         total = total + rp[q]

time: 58.4 us -> 58.5 us (level)
  no operation moved by 1% of the time
where the time goes in v9:
time: 58.5 us; the launch traced here: 58.4 us
  Pallas kernels  57.7 us (99%)
  between operations  0.64 us (1%)
    pallas_call x1, Pallas kernels, on_device(): pl.pallas_call(functools.partial(kernel, ny, nz, nx), out_shape=mids, in_...  55.1 us
    pallas_call x1, Pallas kernels, on_device(): pl.pallas_call(finish, out_shape=mids[0:3] + (cor_shape,), in_specs=[spec...  2.57 us

profile of v9, /device:TPU:1, one launch (start us, length us, event | category | flops | bytes accessed | tf_op | source)
XLA Modules:
  0.0 58.4 jit_solution(10207782622256318086)
XLA Ops:
  0.6 55.1 %shard_map.93 = (f32[7,7,24]{2,1,0:T(8,128)}, f32[32,1536]{1,0:T(8,128)}, f32[32,128]{1,0:T(8,128)}, bf16[128,128]{1,0:T(8,128)(2,1)}, bf16[1536,128]{1,0:T(8,128)(2,1)}, /*index=5*/f32[8,8,24,128]{3,2,1,0:T(8,128)}) custom-call(bf16[24,24,24]{2,1,0:T(8,128)(2,1)} %bitcast.10, f32[7,7,1536]{2,1,0:T(8,128)} %k_hbm.1, bf16[1536,128]{1,0:T(8,128)(2,1)} %w_hbm.1, ...), custom_call_target="tpu_custom_call" | custom-call | flops 600000000 | bytes 4000000 | tf_op jit(solution)/shard_map/pallas_call | solution.py:727
  55.8 2.6 %shard_map.94 = (f32[7,7,24]{2,1,0:T(8,128)}, f32[32,1536]{1,0:T(8,128)}, f32[32,128]{1,0:T(8,128)}, f32[8,8,24,128]{3,2,1,0:T(8,128)}) custom-call(f32[7,7,24]{2,1,0:T(8,128)} %get-tuple-element.14.kg_ref, f32[32,1536]{1,0:T(8,128)} %get-tuple-element.15.left_ref, f32[32,128]{1,0:T(8,128)} %get-tuple-element.16.right_ref, ...), custom_call_target="tpu_custom_call" | custom-call | flops 60000000 | bytes 2500000 | tf_op jit(solution)/shard_map/pallas_call | solution.py:747

commit v10 on v8

--- a/solution.py
+++ b/solution.py
@@ -536,6 +536,23 @@
         term = dot(stack3, part, NT)
         term = term[0:32] + term[32:64] + term[64:96]
         gram = term if gram is None else gram + term
+    cc_copy(3).wait_recv()
+    local_grad(far_x, 1 - k)
+    cor_store = pltpu.make_async_copy(cor, cor_out, s_in.at[6])
+    cor_store.start()
+
+    right = None
+    for q in range(nxk):
+        term = dot(jnp.concatenate(split2(lefts[q]), axis=0), chl[q], NN)
+        right = term if q == 0 else right + term
+    right = right[0:32] + right[32:64]
+    rp[y] = right[:, 0:128] + right[:, 128:256]
+
+    def rp_copy(s):
+        return copy(rp.at[y], rp.at[y], s_rp.at[s], r_rp.at[s], at_y(lax.rem(y + s, ny)))
+
+    loop(1, ny, lambda s: rp_copy(s).start())
+
     for q in range(nxk):
         lsn[:, q] = natural_rows(lefts[q].T)
     natural = lsn[...].reshape(channels, RANK).T
@@ -543,23 +560,6 @@
     ls4[...] = jnp.concatenate([nh, nm, nh, nm], axis=0).T
     ls4_store = pltpu.make_async_copy(ls4, ls4_out, s_in.at[7])
     ls4_store.start()
-
-    cc_copy(3).wait_recv()
-    local_grad(far_x, 1 - k)
-    cor_store = pltpu.make_async_copy(cor, cor_out, s_in.at[6])
-    cor_store.start()
-
-    right = None
-    for q in range(nxk):
-        term = dot(jnp.concatenate(split2(lefts[q]), axis=0), chl[q], NN)
-        right = term if q == 0 else right + term
-    right = right[0:32] + right[32:64]
-    rp[y] = right[:, 0:128] + right[:, 128:256]
-
-    def rp_copy(s):
-        return copy(rp.at[y], rp.at[y], s_rp.at[s], r_rp.at[s], at_y(lax.rem(y + s, ny)))
-
-    loop(1, ny, lambda s: rp_copy(s).start())
 
     row_id = lax.broadcasted_iota(jnp.int32, (RANK, RANK), 0)
     lane_id = lax.broadcasted_iota(jnp.int32, (RANK, RANK), 1)

time: 58.4 us -> 58.5 us (level)
  no operation moved by 1% of the time
where the time goes in v10:
time: 58.5 us; the launch traced here: 58.4 us
  Pallas kernels  57.7 us (99%)
  between operations  0.64 us (1%)
    pallas_call x1, Pallas kernels, on_device(): pl.pallas_call(functools.partial(kernel, ny, nz, nx), out_shape=mids, in_...  55.2 us
    pallas_call x1, Pallas kernels, on_device(): pl.pallas_call(finish, out_shape=mids[0:3] + (cor_shape,), in_specs=[spec...  2.57 us

profile of v10, /device:TPU:1, one launch (start us, length us, event | category | flops | bytes accessed | tf_op | source)
XLA Modules:
  0.0 58.4 jit_solution(1592258075952190655)
XLA Ops:
  0.6 55.2 %shard_map.93 = (f32[7,7,24]{2,1,0:T(8,128)}, f32[32,1536]{1,0:T(8,128)}, f32[32,128]{1,0:T(8,128)}, bf16[128,128]{1,0:T(8,128)(2,1)}, bf16[1536,128]{1,0:T(8,128)(2,1)}, /*index=5*/f32[8,8,24,128]{3,2,1,0:T(8,128)}) custom-call(bf16[24,24,24]{2,1,0:T(8,128)(2,1)} %bitcast.10, f32[7,7,1536]{2,1,0:T(8,128)} %k_hbm.1, bf16[1536,128]{1,0:T(8,128)(2,1)} %w_hbm.1, ...), custom_call_target="tpu_custom_call" | custom-call | flops 600000000 | bytes 4000000 | tf_op jit(solution)/shard_map/pallas_call | solution.py:722
  55.8 2.6 %shard_map.94 = (f32[7,7,24]{2,1,0:T(8,128)}, f32[32,1536]{1,0:T(8,128)}, f32[32,128]{1,0:T(8,128)}, f32[8,8,24,128]{3,2,1,0:T(8,128)}) custom-call(f32[7,7,24]{2,1,0:T(8,128)} %get-tuple-element.14.kg_ref, f32[32,1536]{1,0:T(8,128)} %get-tuple-element.15.left_ref, f32[32,128]{1,0:T(8,128)} %get-tuple-element.16.right_ref, ...), custom_call_target="tpu_custom_call" | custom-call | flops 60000000 | bytes 2500000 | tf_op jit(solution)/shard_map/pallas_call | solution.py:742
